TPU v7x, 512 devices: a whole 4x4x16 slice. The times are simulated.
512 devices in a mesh: cam: 64 (over x_hi, z, core), row: 8 (over y, x_lo).
Axes of the slice: x: 4 (x_hi: 2, x_lo: 2; x = x_hi * 2 + x_lo), y: 4, z: 16, core: 2. Of those that a mesh axis runs over, the one named last changes fastest.
Arguments:
- events: bfloat16 [64, 32, 64, 640], P('cam', None, 'row'), may hold values from -6 to 6
- conv_in: bfloat16 [32, 32, 5, 5], replicated, may hold values from -0.21875 to 0.21875
- bias_in: float32 [32], replicated, may hold values from -3 to 3
- conv_mid: bfloat16 [2, 32, 32, 5, 5], replicated, may hold values from -0.21875 to 0.21875
- bias_mid: float32 [2, 32], replicated, may hold values from -3 to 3
- tap_rows: int32 [2, 48, 64, 4], P(None, None, 'row'), may hold values from 0 to 63, as said below
- tap_weights: float32 [2, 48, 64, 4], P(None, None, 'row'), may hold values from 0 to 1
Outputs:
- volume: bfloat16 [64, 48, 64, 640], P('cam', None, 'row')
- features: bfloat16 [64, 32, 64, 640], P('cam', None, 'row')
Inputs may be any that keep to these rules, and one draw needn't show every extreme that they name: tap_rows[d, p, y, k] lies within 4 rows of y and inside the image.
All inputs are finite; a program needn't handle non-finite values.
Results may differ from a plain program's by a relative error of at most 0.0065.
Values may be sent and summed in bfloat16 or wider, within the bound.
A program may use at most 64 MiB of HBM per device.

v0:
```python
import jax
import jax.numpy as jnp
from jax import lax
from jax.sharding import PartitionSpec as P

BAND = 4


def with_halo(block, sides, width):
    for axis, dim in sides:
        count = lax.axis_size(axis)
        forward = [(i, i + 1) for i in range(count - 1)]
        backward = [(target, source) for source, target in forward]
        low = lax.ppermute(
            lax.slice_in_dim(block, block.shape[dim] - width, None, axis=dim), axis, forward
        )
        high = lax.ppermute(lax.slice_in_dim(block, 0, width, axis=dim), axis, backward)
        block = jnp.concatenate([low, block, high], axis=dim)
    return block


def shifted(block, axis, distance):
    devices = range(lax.axis_size(axis))
    route = [((i - distance) % len(devices), i) for i in devices]
    return lax.ppermute(block, axis, route)


def conv_layer(rows_in, kernel, bias_vec, relu_on):
    result = lax.conv_general_dilated(
        rows_in[None],
        kernel,
        (1, 1),
        ((0, 0), (2, 2)),
        dimension_numbers=("NCHW", "OIHW", "NCHW"),
        preferred_element_type=jnp.float32,
    )[0]
    result = result + bias_vec[:, None, None]
    if relu_on:
        result = jnp.maximum(result, 0.0)
    return result


def match_rows(own_view, partner):
    row_count = own_view.shape[1]
    span = partner.shape[1] - row_count
    products = []
    for shift_row in range(span + 1):
        window = lax.slice_in_dim(partner, shift_row, shift_row + row_count, axis=1)
        products.append(
            jnp.einsum("cyx,cyx->yx", own_view, window, preferred_element_type=jnp.float32)
        )
    return jnp.stack(products, axis=1)


def apply_taps(stacked, tap_rows, tap_weights, first_row):
    row_count = stacked.shape[0]
    span = stacked.shape[1] - 1
    reach = span // 2
    serving = first_row + jnp.arange(row_count, dtype=jnp.int32)
    relative = tap_rows - serving[None, :, None] + reach
    candidate = jnp.arange(span + 1, dtype=jnp.int32)
    weight_table = jnp.sum(
        tap_weights[..., None] * (relative[..., None] == candidate).astype(jnp.float32), axis=2
    )
    return jnp.einsum("pyo,yox->pyx", weight_table, stacked, precision=lax.Precision.HIGHEST)


def local(events, conv_in, bias_in, conv_mid, bias_mid, tap_rows, tap_weights):
    own_events = events[0]
    row_count = own_events.shape[1]
    first_row = lax.axis_index("row") * row_count
    layers = conv_mid.shape[0] + 1
    kernels = [conv_in] + [conv_mid[number] for number in range(layers - 1)]
    biases = [bias_in] + [bias_mid[number] for number in range(layers - 1)]
    current = own_events
    for number in range(layers):
        padded = with_halo(current, (("row", 1),), 2)
        current = conv_layer(padded, kernels[number], biases[number], number < layers - 1).astype(
            jnp.bfloat16
        )
    reach = BAND
    rimmed = with_halo(current, (("row", 1),), reach)
    from_prev = shifted(rimmed, "cam", 1)
    from_next = shifted(rimmed, "cam", -1)
    match_prev = match_rows(current, from_prev)
    match_next = match_rows(current, from_next)
    total = apply_taps(match_prev, tap_rows[0], tap_weights[0], first_row)
    total = total + apply_taps(match_next, tap_rows[1], tap_weights[1], first_row)
    volume = (total / float(current.shape[0])).astype(jnp.bfloat16)
    return (volume[None], current[None])


def solution(mesh):
    in_specs = (
        P("cam", None, "row", None),
        P(),
        P(),
        P(),
        P(),
        P(None, None, "row", None),
        P(None, None, "row", None),
    )
    out_specs = (P("cam", None, "row", None), P("cam", None, "row", None))
    return jax.shard_map(local, mesh=mesh, in_specs=in_specs, out_specs=out_specs, check_vma=False)
```

profile of v0, /device:TPU:97, one launch (start us, length us, event | category | flops | bytes accessed | tf_op | source)
XLA Modules:
  0.0 115.6 jit_solution(15205485978230072494)
XLA Ops:
  0.6 1.2 %fusion.77 = (bf16[32,2,640]{2,1,0:T(2,128)(2,1)S(1)}, bf16[32,2,640]{2,1,0:T(2,128)(2,1)S(1)}) fusion(bf16[32,8,640]{2,1,0:T(8,128)(2,1)} %bitcast.211), kind=kLoop, calls=%fused_computation.135 | loop fusion | bytes 327680 | tf_op jit(solution)/shard_map/slice | solution.py:15
  1.9 3.1 %collective-permute-start = (bf16[32,2,640]{2,1,0:T(2,128)(2,1)S(1)}, bf16[32,2,640]{2,1,0:T(2,128)(2,1)S(1)}, u32[]{:S(2)}, u32[]{:S(2)}) collective-permute-start(bf16[32,2,640]{2,1,0:T(2,128)(2,1)S(1)} %get-tuple-element.47), channel_id=1, source_target_pairs={{0,1},{1,2},{2,3},{3,4},{4,5},{5,6},{6,7},{8,9},{9,10},{10,11},{11... | collective-permute-start | bytes 245768 | tf_op jit(solution)/shard_map/ppermute | solution.py:14
  5.0 1.3 %collective-permute-start.1 = (bf16[32,2,640]{2,1,0:T(2,128)(2,1)S(1)}, bf16[32,2,640]{2,1,0:T(2,128)(2,1)S(1)}, u32[]{:S(2)}, u32[]{:S(2)}) collective-permute-start(bf16[32,2,640]{2,1,0:T(2,128)(2,1)S(1)} %get-tuple-element.48), channel_id=1, source_target_pairs={{1,0},{2,1},{3,2},{4,3},{5,4},{6,5},{7,6},{9,8},{10,9},{11,10},{12... | collective-permute-start | bytes 245768 | tf_op jit(solution)/shard_map/ppermute | solution.py:17
  6.5 3.7 %collective-permute-done.1 = bf16[32,2,640]{2,1,0:T(2,128)(2,1)S(1)} collective-permute-done((bf16[32,2,640]{2,1,0:T(2,128)(2,1)S(1)}, bf16[32,2,640]{2,1,0:T(2,128)(2,1)S(1)}, u32[]{:S(2)}, u32[]{:S(2)}) %collective-permute-start.1) | collective-permute-done | bytes 81952 | tf_op jit(solution)/shard_map/ppermute | solution.py:17
  10.2 1.3 %maximum_bitcast_fusion = bf16[32,12,1,640]{3,1,0,2:T(8,128)(2,1)S(1)} fusion(bf16[32,2,640]{2,1,0:T(2,128)(2,1)S(1)} %collective-permute-done.1, bf16[32,8,640]{2,1,0:T(8,128)(2,1)} %bitcast.212, bf16[32,2,640]{2,1,0:T(2,128)(2,1)S(1)} %collective-permute-done), kind=kLoop, calls=%fused_computation.77 | loop fusion | flops 1474560 | bytes 983040 | tf_op jit(solution)/shard_map/broadcast_in_dim | solution.py:30
  12.8 2.4 %copy.72 = bf16[32,12,1,8,81]{0,3,4,1,2:T(8,128)(2,1)} copy(bf16[32,12,1,8,81]{4,3,1,0,2:T(8,128)(2,1)S(1)} %reshape.118) | data formatting | bytes 995328 | tf_op jit(solution)/shard_map/conv_general_dilated | solution.py:29
  15.2 0.9 slice.145
  16.2 8.6 %fusion.5 = f32[8,8,81,32]{3,1,2,0:T(8,128)} fusion(bf16[32,32,5,5]{1,0,3,2:T(8,128)(2,1)S(1)} %copy-done, bf16[32,12,1,7,4]{0,3,4,1,2:T(8,128)(2,1)S(1)} %slice.145, bf16[32,12,1,8,81]{0,3,4,1,2:T(8,128)(2,1)} %copy.72), kind=kOutput, calls=%fused_computation.24 | convolution fusion | flops 266987520 | bytes 1233920 | tf_op jit(solution)/shard_map/conv_general_dilated | solution.py:29
  24.8 2.2 %copy.73 = f32[8,8,81,32]{2,3,1,0:T(8,128)S(1)} copy(f32[8,8,81,32]{3,1,2,0:T(8,128)} %fusion.5) | data formatting | bytes 1327104 | tf_op jit(solution)/shard_map/conv_general_dilated | solution.py:29
  28.3 4.1 %collective-permute-start.2 = (bf16[32,2,640]{2,0,1:T(8,128)(2,1)S(1)}, bf16[32,2,640]{2,0,1:T(8,128)(2,1)S(1)}, u32[]{:S(2)}, u32[]{:S(2)}) collective-permute-start(bf16[32,2,640]{2,0,1:T(8,128)(2,1)S(1)} %get-tuple-element.45), channel_id=1, source_target_pairs={{0,1},{1,2},{2,3},{3,4},{4,5},{5,6},{6,7},{8,9},{9,10},{10,11},{11... | collective-permute-start | bytes 245768 | tf_op jit(solution)/shard_map/ppermute | solution.py:14
  32.4 1.5 %collective-permute-start.3 = (bf16[32,2,640]{2,0,1:T(8,128)(2,1)S(1)}, bf16[32,2,640]{2,0,1:T(8,128)(2,1)S(1)}, u32[]{:S(2)}, u32[]{:S(2)}) collective-permute-start(bf16[32,2,640]{2,0,1:T(8,128)(2,1)S(1)} %get-tuple-element.46), channel_id=1, source_target_pairs={{1,0},{2,1},{3,2},{4,3},{5,4},{6,5},{7,6},{9,8},{10,9},{11,10},{12... | collective-permute-start | bytes 245768 | tf_op jit(solution)/shard_map/ppermute | solution.py:17
  33.9 4.0 %collective-permute-done.3 = bf16[32,2,640]{2,0,1:T(8,128)(2,1)S(1)} collective-permute-done((bf16[32,2,640]{2,0,1:T(8,128)(2,1)S(1)}, bf16[32,2,640]{2,0,1:T(8,128)(2,1)S(1)}, u32[]{:S(2)}, u32[]{:S(2)}) %collective-permute-start.3) | collective-permute-done | bytes 81952 | tf_op jit(solution)/shard_map/ppermute | solution.py:17
  39.1 1.4 %copy.76 = bf16[32,12,1,8,81]{0,3,4,1,2:T(8,128)(2,1)S(1)} copy(bf16[32,12,1,8,81]{4,3,0,1,2:T(8,128)(2,1)S(1)} %reshape.34) | data formatting | bytes 995328 | tf_op jit(solution)/shard_map/conv_general_dilated | solution.py:29
  40.5 8.0 %fusion.9 = f32[8,8,81,32]{3,1,2,0:T(8,128)} fusion(bf16[32,12,1,7,4]{0,3,4,1,2:T(8,128)(2,1)S(1)} %slice.149, bf16[32,12,1,8,81]{0,3,4,1,2:T(8,128)(2,1)S(1)} %copy.76, bf16[2,32,32,5,5]{2,1,4,3,0:T(8,128)(2,1)} %param.10), kind=kOutput, calls=%fused_computation.27 | convolution fusion | flops 266987520 | bytes 1387520 | tf_op jit(solution)/shard_map/conv_general_dilated | solution.py:29
  48.5 2.2 %copy.77 = f32[8,8,81,32]{2,3,1,0:T(8,128)S(1)} copy(f32[8,8,81,32]{3,1,2,0:T(8,128)} %fusion.9) | data formatting | bytes 1327104 | tf_op jit(solution)/shard_map/conv_general_dilated | solution.py:29
  52.0 3.3 %collective-permute-start.4 = (bf16[32,2,640]{2,0,1:T(8,128)(2,1)S(1)}, bf16[32,2,640]{2,0,1:T(8,128)(2,1)S(1)}, u32[]{:S(2)}, u32[]{:S(2)}) collective-permute-start(bf16[32,2,640]{2,0,1:T(8,128)(2,1)S(1)} %get-tuple-element.43), channel_id=1, source_target_pairs={{0,1},{1,2},{2,3},{3,4},{4,5},{5,6},{6,7},{8,9},{9,10},{10,11},{11... | collective-permute-start | bytes 245768 | tf_op jit(solution)/shard_map/ppermute | solution.py:14
  55.2 1.5 %collective-permute-start.5 = (bf16[32,2,640]{2,0,1:T(8,128)(2,1)S(1)}, bf16[32,2,640]{2,0,1:T(8,128)(2,1)S(1)}, u32[]{:S(2)}, u32[]{:S(2)}) collective-permute-start(bf16[32,2,640]{2,0,1:T(8,128)(2,1)S(1)} %get-tuple-element.44), channel_id=1, source_target_pairs={{1,0},{2,1},{3,2},{4,3},{5,4},{6,5},{7,6},{9,8},{10,9},{11,10},{12... | collective-permute-start | bytes 245768 | tf_op jit(solution)/shard_map/ppermute | solution.py:17
  56.8 3.6 %collective-permute-done.5 = bf16[32,2,640]{2,0,1:T(8,128)(2,1)S(1)} collective-permute-done((bf16[32,2,640]{2,0,1:T(8,128)(2,1)S(1)}, bf16[32,2,640]{2,0,1:T(8,128)(2,1)S(1)}, u32[]{:S(2)}, u32[]{:S(2)}) %collective-permute-start.5) | collective-permute-done | bytes 81952 | tf_op jit(solution)/shard_map/ppermute | solution.py:17
  61.6 1.4 %copy.80 = bf16[32,12,1,8,81]{0,3,4,1,2:T(8,128)(2,1)S(1)} copy(bf16[32,12,1,8,81]{4,3,0,1,2:T(8,128)(2,1)S(1)} %reshape.41) | data formatting | bytes 995328 | tf_op jit(solution)/shard_map/conv_general_dilated | solution.py:29
  63.0 8.0 %fusion.13 = f32[8,8,81,32]{3,1,2,0:T(8,128)} fusion(bf16[32,12,1,7,4]{0,3,4,1,2:T(8,128)(2,1)S(1)} %slice.153, bf16[32,12,1,8,81]{0,3,4,1,2:T(8,128)(2,1)S(1)} %copy.80, bf16[2,32,32,5,5]{2,1,4,3,0:T(8,128)(2,1)} %param.10), kind=kOutput, calls=%fused_computation.30 | convolution fusion | flops 266987520 | bytes 1387520 | tf_op jit(solution)/shard_map/conv_general_dilated | solution.py:29
  71.0 2.2 %copy.81 = f32[8,8,81,32]{2,3,1,0:T(8,128)S(1)} copy(f32[8,8,81,32]{3,1,2,0:T(8,128)} %fusion.13) | data formatting | bytes 1327104 | tf_op jit(solution)/shard_map/conv_general_dilated | solution.py:29
  74.6 4.3 %collective-permute-start.6 = (bf16[32,4,640]{2,0,1:T(8,128)(2,1)S(1)}, bf16[32,4,640]{2,0,1:T(8,128)(2,1)S(1)}, u32[]{:S(2)}, u32[]{:S(2)}) collective-permute-start(bf16[32,4,640]{2,0,1:T(8,128)(2,1)S(1)} %get-tuple-element.41), channel_id=1, source_target_pairs={{0,1},{1,2},{2,3},{3,4},{4,5},{5,6},{6,7},{8,9},{9,10},{10,11},{11... | collective-permute-start | bytes 491528 | tf_op jit(solution)/shard_map/ppermute | solution.py:14
  78.9 1.3 %collective-permute-start.7 = (bf16[32,4,640]{2,0,1:T(8,128)(2,1)S(1)}, bf16[32,4,640]{2,0,1:T(8,128)(2,1)S(1)}, u32[]{:S(2)}, u32[]{:S(2)}) collective-permute-start(bf16[32,4,640]{2,0,1:T(8,128)(2,1)S(1)} %get-tuple-element.42), channel_id=1, source_target_pairs={{1,0},{2,1},{3,2},{4,3},{5,4},{6,5},{7,6},{9,8},{10,9},{11,10},{12... | collective-permute-start | bytes 491528 | tf_op jit(solution)/shard_map/ppermute | solution.py:17
  81.2 3.9 %collective-permute-done.7 = bf16[32,4,640]{2,0,1:T(8,128)(2,1)S(1)} collective-permute-done((bf16[32,4,640]{2,0,1:T(8,128)(2,1)S(1)}, bf16[32,4,640]{2,0,1:T(8,128)(2,1)S(1)}, u32[]{:S(2)}, u32[]{:S(2)}) %collective-permute-start.7) | collective-permute-done | bytes 163872 | tf_op jit(solution)/shard_map/ppermute | solution.py:17
  85.1 0.9 pad_maximum_fusion
  86.0 10.2 %collective-permute-start.8 = (bf16[32,16,640]{2,0,1:T(8,128)(2,1)}, bf16[32,16,640]{2,0,1:T(8,128)(2,1)S(1)}, u32[]{:S(2)}, u32[]{:S(2)}) collective-permute-start(bf16[32,16,640]{2,0,1:T(8,128)(2,1)} %pad_maximum_fusion), channel_id=1, source_target_pairs={{504,0},{0,8},{8,16},{16,24},{24,32},{32,40},{40,48},{48,56},{56,6... | collective-permute-start | bytes 1966088 | tf_op jit(solution)/shard_map/ppermute | solution.py:25
  96.2 2.2 %collective-permute-start.9 = (bf16[32,16,640]{2,0,1:T(8,128)(2,1)}, bf16[32,16,640]{2,0,1:T(8,128)(2,1)S(1)}, u32[]{:S(2)}, u32[]{:S(2)}) collective-permute-start(bf16[32,16,640]{2,0,1:T(8,128)(2,1)} %pad_maximum_fusion), channel_id=1, source_target_pairs={{8,0},{16,8},{24,16},{32,24},{40,32},{48,40},{56,48},{64,56},{72,6... | collective-permute-start | bytes 1966088 | tf_op jit(solution)/shard_map/ppermute | solution.py:25
  100.0 4.1 %collective-permute-done.8 = bf16[32,16,640]{2,0,1:T(8,128)(2,1)S(1)} collective-permute-done((bf16[32,16,640]{2,0,1:T(8,128)(2,1)}, bf16[32,16,640]{2,0,1:T(8,128)(2,1)S(1)}, u32[]{:S(2)}, u32[]{:S(2)}) %collective-permute-start.8) | collective-permute-done | bytes 655392 | tf_op jit(solution)/shard_map/ppermute | solution.py:25
  104.0 5.5 %collective-permute-done.9 = bf16[32,16,640]{2,0,1:T(8,128)(2,1)S(1)} collective-permute-done((bf16[32,16,640]{2,0,1:T(8,128)(2,1)}, bf16[32,16,640]{2,0,1:T(8,128)(2,1)S(1)}, u32[]{:S(2)}, u32[]{:S(2)}) %collective-permute-start.9) | collective-permute-done | bytes 655392 | tf_op jit(solution)/shard_map/ppermute | solution.py:25
  109.5 2.2 %fusion.47 = (f32[8,640]{1,0:T(8,128)S(1)}, f32[8,640]{1,0:T(8,128)S(1)}, f32[8,640]{1,0:T(8,128)S(1)}, f32[8,640]{1,0:T(8,128)S(1)}, f32[8,640]{1,0:T(8,128)S(1...) fusion(bf16[32,16,640]{2,0,1:T(8,128)(2,1)S(1)} %collective-per, ...), kind=kLoop, calls=%fused_computation.65 | loop fusion | flops 9246720 | bytes 6922368 | tf_op jit(solution)/shard_map/cyx,cyx->yx/dot_general | solution.py:50
  112.4 1.0 fusion.61
  113.7 1.0 fusion.26
  (76 shorter events, 11.7 us)
Async XLA Ops:
  0.6 15.5 %copy-start = (bf16[32,32,5,5]{1,0,3,2:T(8,128)(2,1)S(1)}, bf16[32,32,5,5]{1,0,3,2:T(8,128)(2,1)}, u32[]{:S(2)}) copy-start(bf16[32,32,5,5]{1,0,3,2:T(8,128)(2,1)} %param.8) | copy-start | bytes 153604
  1.9 4.6 %collective-permute-start = (bf16[32,2,640]{2,1,0:T(2,128)(2,1)S(1)}, bf16[32,2,640]{2,1,0:T(2,128)(2,1)S(1)}, u32[]{:S(2)}, u32[]{:S(2)}) collective-permute-start(bf16[32,2,640]{2,1,0:T(2,128)(2,1)S(1)} %get-tuple-element.47), channel_id=1, source_target_pairs={{0,1},{1,2},{2,3},{3,4},{4,5},{5,6},{6,7},{8,9},{9,10},{10,11},{11... | collective-permute-start | bytes 245768 | tf_op jit(solution)/shard_map/ppermute | solution.py:14
  5.0 5.2 %collective-permute-start.1 = (bf16[32,2,640]{2,1,0:T(2,128)(2,1)S(1)}, bf16[32,2,640]{2,1,0:T(2,128)(2,1)S(1)}, u32[]{:S(2)}, u32[]{:S(2)}) collective-permute-start(bf16[32,2,640]{2,1,0:T(2,128)(2,1)S(1)} %get-tuple-element.48), channel_id=1, source_target_pairs={{1,0},{2,1},{3,2},{4,3},{5,4},{6,5},{7,6},{9,8},{10,9},{11,10},{12... | collective-permute-start | bytes 245768 | tf_op jit(solution)/shard_map/ppermute | solution.py:17
  24.8 2.2 %copy-start.3 = (pred[8,81]{1,0:T(8,128)(4,1)S(1)}, pred[8,81]{1,0:T(8,128)(4,1)}, u32[]{:S(2)}) copy-start(pred[8,81]{1,0:T(8,128)(4,1)} %constant.29) | copy-start | bytes 1948
  27.2 1.0 copy-start.5
  27.8 6.1 %copy-start.4 = (f32[2,32]{1,0:T(2,128)S(1)}, f32[2,32]{1,0:T(2,128)}, u32[]{:S(2)}) copy-start(f32[2,32]{1,0:T(2,128)} %param.11) | copy-start | bytes 772
  28.3 5.6 %collective-permute-start.2 = (bf16[32,2,640]{2,0,1:T(8,128)(2,1)S(1)}, bf16[32,2,640]{2,0,1:T(8,128)(2,1)S(1)}, u32[]{:S(2)}, u32[]{:S(2)}) collective-permute-start(bf16[32,2,640]{2,0,1:T(8,128)(2,1)S(1)} %get-tuple-element.45), channel_id=1, source_target_pairs={{0,1},{1,2},{2,3},{3,4},{4,5},{5,6},{6,7},{8,9},{9,10},{10,11},{11... | collective-permute-start | bytes 245768 | tf_op jit(solution)/shard_map/ppermute | solution.py:14
  32.4 5.6 %collective-permute-start.3 = (bf16[32,2,640]{2,0,1:T(8,128)(2,1)S(1)}, bf16[32,2,640]{2,0,1:T(8,128)(2,1)S(1)}, u32[]{:S(2)}, u32[]{:S(2)}) collective-permute-start(bf16[32,2,640]{2,0,1:T(8,128)(2,1)S(1)} %get-tuple-element.46), channel_id=1, source_target_pairs={{1,0},{2,1},{3,2},{4,3},{5,4},{6,5},{7,6},{9,8},{10,9},{11,10},{12... | collective-permute-start | bytes 245768 | tf_op jit(solution)/shard_map/ppermute | solution.py:17
  52.0 4.8 %collective-permute-start.4 = (bf16[32,2,640]{2,0,1:T(8,128)(2,1)S(1)}, bf16[32,2,640]{2,0,1:T(8,128)(2,1)S(1)}, u32[]{:S(2)}, u32[]{:S(2)}) collective-permute-start(bf16[32,2,640]{2,0,1:T(8,128)(2,1)S(1)} %get-tuple-element.43), channel_id=1, source_target_pairs={{0,1},{1,2},{2,3},{3,4},{4,5},{5,6},{6,7},{8,9},{9,10},{10,11},{11... | collective-permute-start | bytes 245768 | tf_op jit(solution)/shard_map/ppermute | solution.py:14
  55.2 5.2 %collective-permute-start.5 = (bf16[32,2,640]{2,0,1:T(8,128)(2,1)S(1)}, bf16[32,2,640]{2,0,1:T(8,128)(2,1)S(1)}, u32[]{:S(2)}, u32[]{:S(2)}) collective-permute-start(bf16[32,2,640]{2,0,1:T(8,128)(2,1)S(1)} %get-tuple-element.44), channel_id=1, source_target_pairs={{1,0},{2,1},{3,2},{4,3},{5,4},{6,5},{7,6},{9,8},{10,9},{11,10},{12... | collective-permute-start | bytes 245768 | tf_op jit(solution)/shard_map/ppermute | solution.py:17
  74.1 6.1 %copy-start.1 = (s32[2,48,8,4]{1,3,2,0:T(4,128)S(1)}, s32[2,48,8,4]{1,3,2,0:T(4,128)}, u32[]{:S(2)}) copy-start(s32[2,48,8,4]{1,3,2,0:T(4,128)} %param.12) | copy-start | bytes 36868
  74.1 24.3 %copy-start.2 = (f32[2,48,8,4]{1,3,2,0:T(4,128)S(1)}, f32[2,48,8,4]{1,3,2,0:T(4,128)}, u32[]{:S(2)}) copy-start(f32[2,48,8,4]{1,3,2,0:T(4,128)} %param.13) | copy-start | bytes 36868
  74.6 6.6 %collective-permute-start.6 = (bf16[32,4,640]{2,0,1:T(8,128)(2,1)S(1)}, bf16[32,4,640]{2,0,1:T(8,128)(2,1)S(1)}, u32[]{:S(2)}, u32[]{:S(2)}) collective-permute-start(bf16[32,4,640]{2,0,1:T(8,128)(2,1)S(1)} %get-tuple-element.41), channel_id=1, source_target_pairs={{0,1},{1,2},{2,3},{3,4},{4,5},{5,6},{6,7},{8,9},{9,10},{10,11},{11... | collective-permute-start | bytes 491528 | tf_op jit(solution)/shard_map/ppermute | solution.py:14
  78.9 6.2 %collective-permute-start.7 = (bf16[32,4,640]{2,0,1:T(8,128)(2,1)S(1)}, bf16[32,4,640]{2,0,1:T(8,128)(2,1)S(1)}, u32[]{:S(2)}, u32[]{:S(2)}) collective-permute-start(bf16[32,4,640]{2,0,1:T(8,128)(2,1)S(1)} %get-tuple-element.42), channel_id=1, source_target_pairs={{1,0},{2,1},{3,2},{4,3},{5,4},{6,5},{7,6},{9,8},{10,9},{11,10},{12... | collective-permute-start | bytes 491528 | tf_op jit(solution)/shard_map/ppermute | solution.py:17
  86.0 18.0 %collective-permute-start.8 = (bf16[32,16,640]{2,0,1:T(8,128)(2,1)}, bf16[32,16,640]{2,0,1:T(8,128)(2,1)S(1)}, u32[]{:S(2)}, u32[]{:S(2)}) collective-permute-start(bf16[32,16,640]{2,0,1:T(8,128)(2,1)} %pad_maximum_fusion), channel_id=1, source_target_pairs={{504,0},{0,8},{8,16},{16,24},{24,32},{32,40},{40,48},{48,56},{56,6... | collective-permute-start | bytes 1966088 | tf_op jit(solution)/shard_map/ppermute | solution.py:25
  96.2 13.3 %collective-permute-start.9 = (bf16[32,16,640]{2,0,1:T(8,128)(2,1)}, bf16[32,16,640]{2,0,1:T(8,128)(2,1)S(1)}, u32[]{:S(2)}, u32[]{:S(2)}) collective-permute-start(bf16[32,16,640]{2,0,1:T(8,128)(2,1)} %pad_maximum_fusion), channel_id=1, source_target_pairs={{8,0},{16,8},{24,16},{32,24},{40,32},{48,40},{56,48},{64,56},{72,6... | collective-permute-start | bytes 1966088 | tf_op jit(solution)/shard_map/ppermute | solution.py:25
where the time goes:
time: 116 us
  starting transfers between devices  32.7 us (28%)
  matrix products  26.6 us (23%)
  waiting for transfers between devices  25.9 us (22%)
  local copies, waits for them, and re-layouts  23.5 us (20%)
  other arithmetic  5.62 us (5%)
  between operations  1.29 us (1%)
    conv_general_dilated x3, matrix products, conv_layer(): lax.conv_general_dilated(rows_in[None], kernel, (1, 1), ((0, 0), (2, 2)),...  24.6 us
    conv_general_dilated x18, local copies, waits for them, and re-layouts, conv_layer(): lax.conv_general_dilated(rows_in[None], kernel, (1, 1), ((0, 0), (2, 2)),...  18.1 us
    ppermute x4, waiting for transfers between devices, with_halo(): lax.ppermute(lax.slice_in_dim(block, 0, width, axis=dim), axis, backward)  15.3 us
    ppermute x4, starting transfers between devices, with_halo(): lax.ppermute(lax.slice_in_dim(block, block.shape[dim] - width, None, axis...  14.8 us
    ppermute x2, starting transfers between devices, shifted(): return lax.ppermute(block, axis, route)  12.4 us
    ppermute x2, waiting for transfers between devices, shifted(): return lax.ppermute(block, axis, route)  9.56 us
    ppermute x4, starting transfers between devices, with_halo(): lax.ppermute(lax.slice_in_dim(block, 0, width, axis=dim), axis, backward)  5.57 us
  transfers between devices with their start and end apart: 10, of which 8 were waited for; matrix products, arithmetic and copies ran while one was open for 1% of the time, Pallas kernels for 0%

commit v1 on v0

v1 whole, which is shorter than its diff:
```python
import functools

import jax
import jax.numpy as jnp
from jax import lax
from jax.experimental import pallas as pl
from jax.experimental.pallas import tpu as pltpu
from jax.sharding import PartitionSpec as P

MESH = pl.DeviceIdType.MESH
F32 = jnp.float32
BF16 = jnp.bfloat16

CH = 32
BANDS = 8
ROWS = 8
COLS = 640
STRIP = COLS // BANDS
HALO = 6
LANES = 128
TILES = COLS // LANES
BLK = CH * ROWS
EDGE = 2 * CH
KROWS = BLK + 2 * EDGE
PLANES = 48
SPAN = 9
REACH = 4
MROWS = 2 * SPAN * ROWS


def lane_ids(shape):
    return lax.broadcasted_iota(jnp.int32, shape, 1)


def row_ids(shape):
    return lax.broadcasted_iota(jnp.int32, shape, 0)


def roll(value, shift):
    shift = shift % value.shape[1]
    return value if shift == 0 else pltpu.roll(value, shift, 1)


def row_major_perm():
    shape = (BLK, BLK)
    i, j = row_ids(shape), lane_ids(shape)
    return ((i & 31) * ROWS + (i >> 5) == j).astype(BF16)


def channel_major_perm():
    shape = (BLK, BLK)
    i, j = row_ids(shape), lane_ids(shape)
    return ((i & 7) * CH + (i >> 3) == j).astype(BF16)


def window_of(tiles, strip):
    start = STRIP * strip - HALO
    first = start // LANES
    off = start - first * LANES
    shape = tiles[0].shape
    low = roll(tiles[first], -off) if first >= 0 else jnp.zeros(shape, F32)
    if LANES - off >= STRIP + 2 * HALO:
        return low
    high = roll(tiles[first + 1], -off) if first + 1 < TILES else jnp.zeros(shape, F32)
    return jnp.where(lane_ids(shape) < LANES - off, low, high)


def unwindow(get, tile):
    out = None
    for strip in range(BANDS):
        lo = max(STRIP * strip, LANES * tile) - LANES * tile
        hi = min(STRIP * (strip + 1), LANES * (tile + 1)) - LANES * tile
        if lo < hi:
            value = roll(get(strip), STRIP * strip - HALO - LANES * tile)
            out = value if out is None else jnp.where(lane_ids(value.shape) >= lo, value, out)
    return out


def build_taps(w, t_ref):
    for dx in range(5):
        pieces = [w(dy, dx).astype(F32) for dy in range(5)]
        base = jnp.concatenate(pieces + [jnp.zeros((CH, KROWS - 5 * CH), F32)], axis=1)
        for y in range(ROWS):
            t_ref[CH * y : CH * (y + 1), KROWS * dx : KROWS * (dx + 1)] = roll(base, CH * y).astype(BF16)


def bias_column(bias_row, channel_major):
    shape = (BLK, CH)
    i = row_ids(shape)
    owner = (i >> 3) if channel_major else (i & 31)
    spread = jnp.where(owner == lane_ids(shape), jnp.broadcast_to(bias_row, shape), 0.0)
    return jnp.broadcast_to(jnp.sum(spread, axis=1, keepdims=True), (BLK, LANES))


def kernel(
    cams,
    ev_ref, w1_ref, wm_ref, b1_ref, bm_ref, rows_ref, wts_ref,
    vol_ref, feat_ref,
    win, x1, x2, x3, t1, t2, t3, bias, fblk, frx, fown, fpart, fback, macc, msend, mrecv, tab,
    s1_send, s1_recv, f_send, f_recv, o_send, o_recv, m_send, m_recv,
):
    cam = lax.axis_index("cam")
    me = lax.axis_index("row")
    nxt = (lax.rem(cam + 1, cams), me)
    prv = (lax.rem(cam + cams - 1, cams), me)
    peers = [lax.rem(me + k, BANDS) for k in range(1, BANDS)]

    barrier = pltpu.get_barrier_semaphore()
    for peer in peers:
        pl.semaphore_signal(barrier, inc=1, device_id=(cam, peer), device_id_type=MESH)
    for peer in (nxt, prv):
        pl.semaphore_signal(barrier, inc=1, device_id=peer, device_id_type=MESH)

    ev = jnp.dot(row_major_perm(), ev_ref[...], preferred_element_type=F32)
    tiles = [ev[:, LANES * t : LANES * (t + 1)] for t in range(TILES)]
    for strip in range(BANDS):
        win[strip] = window_of(tiles, strip).astype(BF16)

    pl.semaphore_wait(barrier, BANDS + 1)

    def block_rows(b):
        return pl.ds(pl.multiple_of(EDGE + b * BLK, EDGE), BLK)

    def s1_copy(dst, src_row):
        return pltpu.make_async_remote_copy(
            src_ref=win.at[dst],
            dst_ref=x1.at[block_rows(src_row)],
            send_sem=s1_send.at[dst],
            recv_sem=s1_recv.at[src_row],
            device_id=(cam, dst),
            device_id_type=MESH,
        )

    for peer in peers:
        s1_copy(peer, me).start()
    x1[block_rows(me)] = win[me]

    zero_edge = jnp.zeros((EDGE, LANES), BF16)
    for x in (x1, x2, x3):
        x[0:EDGE] = zero_edge
        x[EDGE + BANDS * BLK :] = zero_edge
    build_taps(lambda dy, dx: w1_ref[dy, dx], t1)
    build_taps(lambda dy, dx: wm_ref[0, dy, dx], t2)
    build_taps(lambda dy, dx: wm_ref[1, dy, dx], t3)
    perm = channel_major_perm()
    for dx in range(5):
        cols = slice(KROWS * dx, KROWS * (dx + 1))
        t3[:, cols] = jnp.dot(perm, t3[:, cols], preferred_element_type=F32).astype(BF16)
    bias[0] = bias_column(b1_ref[...], False)
    bias[1] = bias_column(bm_ref[0:1], False)
    bias[2] = bias_column(bm_ref[1:2], True)
    for d in range(2):
        fpart[d, :, 0:ROWS] = jnp.zeros((CH, ROWS, LANES), F32)
        fpart[d, :, ROWS * (BANDS + 1) :] = jnp.zeros((CH, ROWS, LANES), F32)

    first = me * ROWS
    shape = (ROWS, LANES)
    pick = (
        ((row_ids((PLANES * ROWS, 4 * LANES)) & 7) * 64 + (row_ids((PLANES * ROWS, 4 * LANES)) >> 3))
        == lane_ids((PLANES * ROWS, 4 * LANES))
    ).astype(BF16)
    serving = first + row_ids((ROWS, PLANES)) - REACH
    parts = []
    for d in range(2):
        for o in range(SPAN):
            total = jnp.zeros((ROWS, PLANES), F32)
            for k in range(4):
                hit = rows_ref[d, :, k] == serving + o
                total = total + jnp.where(hit, wts_ref[d, :, k], 0.0)
            total = total * (1.0 / CH)
            wide = jnp.concatenate([total, jnp.zeros((ROWS, 64 - PLANES), F32)], axis=1)
            wide = jnp.concatenate([wide, wide], axis=1)
            half = lane_ids(shape) >> 6
            parts.append(
                jnp.concatenate(
                    [jnp.where(row_ids(shape) == 2 * j + half, wide, 0.0) for j in range(4)], axis=1
                )
            )
    table = jnp.concatenate(parts, axis=0)
    high = table.astype(BF16)
    low = (table - high.astype(F32)).astype(BF16)
    for n, piece in enumerate((high, low)):
        tab[n] = lax.dot_general(
            pick, piece, (((1,), (1,)), ((), ())), preferred_element_type=F32
        ).astype(BF16)

    for k in range(1, BANDS):
        s1_copy(peers[0], lax.rem(me + BANDS - k, BANDS)).wait_recv()

    column = lane_ids((1, LANES)) + me * STRIP - HALO
    inside = jnp.logical_and(column >= 0, column < COLS)

    def conv(x, t, pair):
        halves = []
        for b in (2 * pair, 2 * pair + 1):
            rows = x[BLK * b : BLK * b + KROWS].astype(F32)
            halves.append(
                jnp.concatenate([roll(rows, 2 - dx).astype(BF16) for dx in range(5)], axis=0)
            )
        return jnp.dot(t[...], jnp.concatenate(halves, axis=1), preferred_element_type=F32)

    def hidden(x, t, number, y, pair):
        out = conv(x, t, pair)
        for h in range(2):
            value = jnp.maximum(out[:, LANES * h : LANES * (h + 1)] + bias[number], 0.0)
            start = EDGE + BLK * (2 * pair + h)
            y[start : start + BLK] = jnp.where(inside, value, 0.0).astype(BF16)

    def f_copy(d, b):
        return pltpu.make_async_remote_copy(
            src_ref=fblk.at[b],
            dst_ref=frx.at[d, b],
            send_sem=f_send.at[d, b],
            recv_sem=f_recv.at[d, b],
            device_id=nxt if d == 0 else prv,
            device_id_type=MESH,
        )

    def last(pair):
        out = conv(x3, t3, pair)
        for h in range(2):
            b = 2 * pair + h
            value = (out[:, LANES * h : LANES * (h + 1)] + bias[2]).astype(BF16)
            fblk[b] = value
            fown[:, ROWS * b : ROWS * (b + 1)] = value.astype(F32).reshape(CH, ROWS, LANES)
            for d in range(2):
                f_copy(d, b).start()

    pairs = BANDS // 2
    for step in range(pairs + 2):
        if step < pairs:
            hidden(x1, t1, 0, x2, step)
        if 0 <= step - 1 < pairs:
            hidden(x2, t2, 1, x3, step - 1)
        if 0 <= step - 2 < pairs:
            last(step - 2)

    def o_copy(dst, strip):
        return pltpu.make_async_remote_copy(
            src_ref=fblk.at[dst],
            dst_ref=fback.at[strip],
            send_sem=o_send.at[dst],
            recv_sem=o_recv.at[strip],
            device_id=(cam, dst),
            device_id_type=MESH,
        )

    for peer in peers:
        o_copy(peer, me).start()
    fback[me] = fblk[me]

    def m_copy(dst, strip):
        return pltpu.make_async_remote_copy(
            src_ref=msend.at[dst],
            dst_ref=mrecv.at[strip],
            send_sem=m_send.at[dst],
            recv_sem=m_recv.at[strip],
            device_id=(cam, dst),
            device_id_type=MESH,
        )

    def arrive(b):
        for d in range(2):
            f_copy(d, b).wait_recv()
            fpart[d, :, ROWS * (b + 1) : ROWS * (b + 2)] = (
                frx[d, b].astype(F32).reshape(CH, ROWS, LANES)
            )

    def match(b):
        for d in range(2):

            def channel(c, acc):
                own = fown[c, ROWS * b : ROWS * (b + 1)]
                return tuple(
                    acc[o] + own * fpart[d, c, ROWS * (b + 1) + o - REACH : ROWS * (b + 2) + o - REACH]
                    for o in range(SPAN)
                )

            acc = lax.fori_loop(
                0, CH, channel, tuple(jnp.zeros((ROWS, LANES), F32) for _ in range(SPAN)), unroll=8
            )
            for o in range(SPAN):
                start = (d * SPAN + o) * ROWS
                macc[start : start + ROWS] = acc[o]
        msend[b] = macc[...].astype(BF16)

        @pl.when(me != b)
        def _():
            m_copy(b, me).start()

    arrive(0)
    for b in range(BANDS):
        if b + 1 < BANDS:
            arrive(b + 1)
        match(b)
    mrecv[me] = msend[me]

    for k in range(1, BANDS):
        o_copy(peers[0], lax.rem(me + BANDS - k, BANDS)).wait_recv()
    for t in range(TILES):
        feat_ref[:, LANES * t : LANES * (t + 1)] = unwindow(
            lambda s: fback[s].astype(F32), t
        ).astype(BF16)

    for k in range(1, BANDS):
        m_copy(peers[0], lax.rem(me + BANDS - k, BANDS)).wait_recv()
    for t in range(TILES):
        values = unwindow(lambda s: mrecv[s].astype(F32), t).astype(BF16)
        out = jnp.dot(tab[0], values, preferred_element_type=F32)
        out = out + jnp.dot(tab[1], values, preferred_element_type=F32)
        vol_ref[:, LANES * t : LANES * (t + 1)] = out.astype(BF16)

    for peer in peers:
        s1_copy(peer, me).wait_send()
        o_copy(peer, me).wait_send()
        m_copy(peer, me).wait_send()
    for b in range(BANDS):
        for d in range(2):
            f_copy(d, b).wait_send()


def local(cams, events, conv_in, bias_in, conv_mid, bias_mid, tap_rows, tap_weights):
    dma = pltpu.SemaphoreType.DMA
    vmem = pl.BlockSpec(memory_space=pltpu.VMEM)
    padded = (BANDS * BLK + 2 * EDGE, LANES)
    taps = (BLK, 5 * KROWS)
    vol, feat = pl.pallas_call(
        functools.partial(kernel, cams),
        out_shape=(
            jax.ShapeDtypeStruct((PLANES * ROWS, COLS), BF16),
            jax.ShapeDtypeStruct((BLK, COLS), BF16),
        ),
        in_specs=[vmem] * 7,
        out_specs=(vmem, vmem),
        scratch_shapes=[
            pltpu.VMEM((BANDS, BLK, LANES), BF16),
            pltpu.VMEM(padded, BF16),
            pltpu.VMEM(padded, BF16),
            pltpu.VMEM(padded, BF16),
            pltpu.VMEM(taps, BF16),
            pltpu.VMEM(taps, BF16),
            pltpu.VMEM(taps, BF16),
            pltpu.VMEM((3, BLK, LANES), F32),
            pltpu.VMEM((BANDS, BLK, LANES), BF16),
            pltpu.VMEM((2, BANDS, BLK, LANES), BF16),
            pltpu.VMEM((CH, ROWS * BANDS, LANES), F32),
            pltpu.VMEM((2, CH, ROWS * (BANDS + 2), LANES), F32),
            pltpu.VMEM((BANDS, BLK, LANES), BF16),
            pltpu.VMEM((MROWS, LANES), F32),
            pltpu.VMEM((BANDS, MROWS, LANES), BF16),
            pltpu.VMEM((BANDS, MROWS, LANES), BF16),
            pltpu.VMEM((2, PLANES * ROWS, MROWS), BF16),
            dma((BANDS,)), dma((BANDS,)),
            dma((2, BANDS)), dma((2, BANDS)),
            dma((BANDS,)), dma((BANDS,)),
            dma((BANDS,)), dma((BANDS,)),
        ],
        compiler_params=pltpu.CompilerParams(
            collective_id=0, has_side_effects=True, vmem_limit_bytes=40 * 1024 * 1024
        ),
    )(
        events.reshape(BLK, COLS),
        conv_in.transpose(2, 3, 0, 1),
        conv_mid.transpose(0, 3, 4, 1, 2),
        bias_in.reshape(1, CH),
        bias_mid,
        tap_rows.transpose(0, 2, 3, 1),
        tap_weights.transpose(0, 2, 3, 1),
    )
    return vol.reshape(1, PLANES, ROWS, COLS), feat.reshape(1, CH, ROWS, COLS)


def solution(mesh):
    in_specs = (
        P("cam", None, "row", None),
        P(),
        P(),
        P(),
        P(),
        P(None, None, "row", None),
        P(None, None, "row", None),
    )
    out_specs = (P("cam", None, "row", None), P("cam", None, "row", None))
    return jax.shard_map(
        functools.partial(local, mesh.shape["cam"]),
        mesh=mesh,
        in_specs=in_specs,
        out_specs=out_specs,
        check_vma=False,
    )
```

time: 116 us -> 46.9 us (0.40)
  the two profiles are of different devices: /device:TPU:97 before, /device:TPU:2 now
where the time goes in v1:
time: 46.9 us; the launch traced here: 46.5 us
  Pallas kernels  39.3 us (84%)
  local copies, waits for them, and re-layouts  6.59 us (14%)
  between operations  0.66 us (1%)
    pallas_call x1, Pallas kernels, local(): pl.pallas_call(functools.partial(kernel, cams), out_shape=(jax.ShapeDtype...  39.3 us
    unnamed x16, local copies, waits for them, and re-layouts  6.59 us

profile of v1, /device:TPU:2, one launch (start us, length us, event | category | flops | bytes accessed | tf_op | source)
XLA Modules:
  0.0 46.5 jit_solution(7583621383784373787)
XLA Ops:
  0.6 0.0 copy-start.5
  0.6 0.0 copy-start.6
  0.7 0.7 %copy-done.5 = f32[2,32]{1,0:T(2,128)S(1)} copy-done((f32[2,32]{1,0:T(2,128)S(1)}, f32[2,32]{1,0:T(2,128)}, u32[]{:S(2)}) %copy-start.5) | copy-done | bytes 280
  1.3 0.0 copy-done.6
  1.3 0.0 copy-start
  1.3 1.0 %copy-done = bf16[2,32,32,5,5]{2,1,4,3,0:T(8,128)(2,1)S(1)} copy-done((bf16[2,32,32,5,5]{2,1,4,3,0:T(8,128)(2,1)S(1)}, bf16[2,32,32,5,5]{2,1,4,3,0:T(8,128)(2,1)}, u32[]{:S(2)}) %copy-start) | copy-done | bytes 102424
  2.3 0.0 copy-start.1
  2.3 1.0 %copy-done.1 = bf16[1,32,8,640]{3,2,1,0:T(8,128)(2,1)S(1)} copy-done((bf16[1,32,8,640]{3,2,1,0:T(8,128)(2,1)S(1)}, bf16[1,32,8,640]{3,2,1,0:T(8,128)(2,1)}, u32[]{:S(2)}) %copy-start.1) | copy-done | bytes 327704
  3.3 0.0 copy-start.2
  3.3 0.9 %copy-done.2 = bf16[32,32,5,5]{1,0,3,2:T(8,128)(2,1)S(1)} copy-done((bf16[32,32,5,5]{1,0,3,2:T(8,128)(2,1)S(1)}, bf16[32,32,5,5]{1,0,3,2:T(8,128)(2,1)}, u32[]{:S(2)}) %copy-start.2) | copy-done | bytes 51224
  4.2 0.0 copy-start.3
  4.2 0.8 %copy-done.3 = s32[2,48,8,4]{1,3,2,0:T(4,128)S(1)} copy-done((s32[2,48,8,4]{1,3,2,0:T(4,128)S(1)}, s32[2,48,8,4]{1,3,2,0:T(4,128)}, u32[]{:S(2)}) %copy-start.3) | copy-done | bytes 12312
  5.0 0.0 copy-start.4
  5.0 0.8 %copy-done.4 = f32[2,48,8,4]{1,3,2,0:T(4,128)S(1)} copy-done((f32[2,48,8,4]{1,3,2,0:T(4,128)S(1)}, f32[2,48,8,4]{1,3,2,0:T(4,128)}, u32[]{:S(2)}) %copy-start.4) | copy-done | bytes 12312
  5.7 39.3 %shard_map.86 = (bf16[384,640]{1,0:T(8,128)(2,1)S(1)}, bf16[256,640]{1,0:T(8,128)(2,1)S(1)}) custom-call(bf16[256,640]{1,0:T(8,128)(2,1)S(1)} %bitcast.10, bf16[5,5,32,32]{3,2,1,0:T(8,128)(2,1)S(1)} %bitcast.12, bf16[2,5,5,32,32]{4,3,2,1,0:T(8,128)(2,1)S(1)} %bitcast.9, f32[1,32]{1,0:T(1,128)S(1)} %bitcast.15, f32[2,32]{1,0:T(2,128)S(1)} %copy-done.5, ...), custom_call_target="tpu_custom_call" | custom-call | tf_op jit(solution)/shard_map/pallas_call | solution.py:327
  45.0 0.8 %copy.11 = bf16[1,48,8,640]{3,2,1,0:T(8,128)(2,1)} copy(bf16[1,48,8,640]{3,2,1,0:T(8,128)(2,1)S(1)} %bitcast.8) | data formatting | bytes 983040
  45.8 0.7 %copy.12 = bf16[1,32,8,640]{3,2,1,0:T(8,128)(2,1)} copy(bf16[1,32,8,640]{3,2,1,0:T(8,128)(2,1)S(1)} %bitcast.11) | data formatting | bytes 655360
Async XLA Ops:
  0.6 0.7 %copy-start.5 = (f32[2,32]{1,0:T(2,128)S(1)}, f32[2,32]{1,0:T(2,128)}, u32[]{:S(2)}) copy-start(f32[2,32]{1,0:T(2,128)} %bm_ref.1) | copy-start | bytes 772
  0.6 0.7 %copy-start.6 = (f32[32]{0:T(128)S(1)}, f32[32]{0:T(128)}, u32[]{:S(2)}) copy-start(f32[32]{0:T(128)} %param.9) | copy-start | bytes 388
  1.3 1.0 %copy-start = (bf16[2,32,32,5,5]{2,1,4,3,0:T(8,128)(2,1)S(1)}, bf16[2,32,32,5,5]{2,1,4,3,0:T(8,128)(2,1)}, u32[]{:S(2)}) copy-start(bf16[2,32,32,5,5]{2,1,4,3,0:T(8,128)(2,1)} %param.10) | copy-start | bytes 307204
  2.3 1.0 %copy-start.1 = (bf16[1,32,8,640]{3,2,1,0:T(8,128)(2,1)S(1)}, bf16[1,32,8,640]{3,2,1,0:T(8,128)(2,1)}, u32[]{:S(2)}) copy-start(bf16[1,32,8,640]{3,2,1,0:T(8,128)(2,1)} %param.7) | copy-start | bytes 983044
  3.3 0.9 %copy-start.2 = (bf16[32,32,5,5]{1,0,3,2:T(8,128)(2,1)S(1)}, bf16[32,32,5,5]{1,0,3,2:T(8,128)(2,1)}, u32[]{:S(2)}) copy-start(bf16[32,32,5,5]{1,0,3,2:T(8,128)(2,1)} %param.8) | copy-start | bytes 153604
  4.2 0.8 %copy-start.3 = (s32[2,48,8,4]{1,3,2,0:T(4,128)S(1)}, s32[2,48,8,4]{1,3,2,0:T(4,128)}, u32[]{:S(2)}) copy-start(s32[2,48,8,4]{1,3,2,0:T(4,128)} %param.12) | copy-start | bytes 36868
  5.0 0.8 %copy-start.4 = (f32[2,48,8,4]{1,3,2,0:T(4,128)S(1)}, f32[2,48,8,4]{1,3,2,0:T(4,128)}, u32[]{:S(2)}) copy-start(f32[2,48,8,4]{1,3,2,0:T(4,128)} %param.13) | copy-start | bytes 36868

commit v2 on v1

v2 whole, which is shorter than its diff:
```python
import functools

import jax
import jax.numpy as jnp
from jax import lax
from jax.experimental import pallas as pl
from jax.experimental.pallas import tpu as pltpu
from jax.sharding import PartitionSpec as P

MESH = pl.DeviceIdType.MESH
F32 = jnp.float32
BF16 = jnp.bfloat16

CH = 32
BANDS = 8
ROWS = 8
COLS = 640
STRIP = COLS // BANDS
HALO = 6
LANES = 128
TILES = COLS // LANES
BLK = CH * ROWS
EDGE = 2 * CH
KROWS = BLK + 2 * EDGE
PLANES = 48
SPAN = 9
REACH = 4
MROWS = SPAN * ROWS
GROUPS = 4
PACK = 5
FROWS = GROUPS * PACK * ROWS
MPACK = 6 * ROWS


def lane_ids(shape):
    return lax.broadcasted_iota(jnp.int32, shape, 1)


def row_ids(shape):
    return lax.broadcasted_iota(jnp.int32, shape, 0)


def roll(value, shift):
    shift = shift % value.shape[1]
    return value if shift == 0 else pltpu.roll(value, shift, 1)


def row_major_perm():
    shape = (BLK, BLK)
    i, j = row_ids(shape), lane_ids(shape)
    return ((i & 31) * ROWS + (i >> 5) == j).astype(BF16)


def channel_major_perm():
    shape = (BLK, BLK)
    i, j = row_ids(shape), lane_ids(shape)
    return ((i & 7) * CH + (i >> 3) == j).astype(BF16)


def window_of(tiles, strip):
    start = STRIP * strip - HALO
    first = start // LANES
    off = start - first * LANES
    shape = tiles[0].shape
    low = roll(tiles[first], -off) if first >= 0 else jnp.zeros(shape, F32)
    if LANES - off >= STRIP + 2 * HALO:
        return low
    high = roll(tiles[first + 1], -off) if first + 1 < TILES else jnp.zeros(shape, F32)
    return jnp.where(lane_ids(shape) < LANES - off, low, high)


def place(pieces, tile):
    out = None
    for get, lane, column, count in pieces:
        lo = max(column, LANES * tile) - LANES * tile
        hi = min(column + count, LANES * (tile + 1)) - LANES * tile
        if lo < hi:
            value = roll(get(), column - LANES * tile - lane)
            out = value if out is None else jnp.where(lane_ids(value.shape) >= lo, value, out)
    return out


def pack_features(value):
    lane = lane_ids((ROWS, LANES))
    out = []
    for g in range(GROUPS):
        tail = None
        for k in range(4):
            even = roll(value[8 * g + 2 * k], -HALO)
            odd = roll(value[8 * g + 2 * k + 1], 64 - HALO)
            out.append(jnp.where(lane < 64, even, odd))
            both = roll(jnp.where(lane < 64, odd, even), 16 * k)
            tail = both if tail is None else jnp.where((lane & 63) >= 16 * k, both, tail)
        out.append(tail)
    return out


def build_taps(w, t_ref):
    for dx in range(5):
        pieces = [w(dy, dx).astype(F32) for dy in range(5)]
        base = jnp.concatenate(pieces + [jnp.zeros((CH, KROWS - 5 * CH), F32)], axis=1)
        for y in range(ROWS):
            t_ref[CH * y : CH * (y + 1), KROWS * dx : KROWS * (dx + 1)] = roll(base, CH * y).astype(BF16)


def bias_column(bias_row, channel_major):
    shape = (BLK, CH)
    i = row_ids(shape)
    owner = (i >> 3) if channel_major else (i & 31)
    spread = jnp.where(owner == lane_ids(shape), jnp.broadcast_to(bias_row, shape), 0.0)
    return jnp.broadcast_to(jnp.sum(spread, axis=1, keepdims=True), (BLK, LANES))


def kernel(
    cams,
    ev_hbm, w1_hbm, wm_hbm, b1_hbm, bm_hbm, rows_hbm, wts_hbm,
    vol_ref, feat_ref,
    ev_ref, w1_ref, wm_ref, b1_ref, bm_ref, rows_ref, wts_ref,
    win, x1, x2, x3, t1, t2, t3, bias, fblk, frx, fown, fpart, fback, msend, mrecv, mval, featf, wide, tab,
    in_sem, s1_send, s1_recv, f_send, f_recv, o_send, o_recv, m_send, m_recv,
):
    cam = lax.axis_index("cam")
    me = lax.axis_index("row")
    odd = lax.rem(cam, 2)
    far = (lax.rem(cam + cams - 1 + 2 * odd, cams), me)
    near = (cam + 1 - 2 * odd, me)
    peers = [lax.rem(me + k, BANDS) for k in range(1, BANDS)]

    barrier = pltpu.get_barrier_semaphore()
    for peer in peers:
        pl.semaphore_signal(barrier, inc=1, device_id=(cam, peer), device_id_type=MESH)
    for peer in (far, near):
        pl.semaphore_signal(barrier, inc=1, device_id=peer, device_id_type=MESH)
    loads = [
        pltpu.make_async_copy(src, dst, in_sem.at[n])
        for n, (src, dst) in enumerate(
            (
                (ev_hbm, ev_ref), (w1_hbm, w1_ref), (wm_hbm, wm_ref), (b1_hbm, b1_ref),
                (bm_hbm, bm_ref), (rows_hbm, rows_ref), (wts_hbm, wts_ref),
            )
        )
    ]
    for load in loads:
        load.start()
    loads[0].wait()

    ev = jnp.dot(row_major_perm(), ev_ref[...], preferred_element_type=F32)
    tiles = [ev[:, LANES * t : LANES * (t + 1)] for t in range(TILES)]
    for strip in range(BANDS):
        win[strip] = window_of(tiles, strip).astype(BF16)

    pl.semaphore_wait(barrier, BANDS + 1)

    def block_rows(b):
        return pl.ds(pl.multiple_of(EDGE + b * BLK, EDGE), BLK)

    def s1_copy(dst, src_row):
        return pltpu.make_async_remote_copy(
            src_ref=win.at[dst],
            dst_ref=x1.at[block_rows(src_row)],
            send_sem=s1_send.at[dst],
            recv_sem=s1_recv.at[src_row],
            device_id=(cam, dst),
            device_id_type=MESH,
        )

    for peer in peers:
        s1_copy(peer, me).start()
    x1[block_rows(me)] = win[me]

    for load in loads[1:]:
        load.wait()

    zero_edge = jnp.zeros((EDGE, LANES), BF16)
    for x in (x1, x2, x3):
        x[0:EDGE] = zero_edge
        x[EDGE + BANDS * BLK :] = zero_edge
    build_taps(lambda dy, dx: w1_ref[dy, dx], t1)
    build_taps(lambda dy, dx: wm_ref[0, dy, dx], t2)
    build_taps(lambda dy, dx: wm_ref[1, dy, dx], t3)
    perm = channel_major_perm()
    for dx in range(5):
        cols = slice(KROWS * dx, KROWS * (dx + 1))
        t3[:, cols] = jnp.dot(perm, t3[:, cols], preferred_element_type=F32).astype(BF16)
    bias[0] = bias_column(b1_ref[...], False)
    bias[1] = bias_column(bm_ref[0:1], False)
    bias[2] = bias_column(bm_ref[1:2], True)
    for d in range(2):
        edge = jnp.zeros((GROUPS * PACK, ROWS, LANES), F32)
        fpart[d, :, 0:ROWS] = edge
        fpart[d, :, ROWS * (BANDS + 1) :] = edge

    first = me * ROWS
    shape = (ROWS, LANES)
    pick = (
        ((row_ids((PLANES * ROWS, 4 * LANES)) & 7) * 64 + (row_ids((PLANES * ROWS, 4 * LANES)) >> 3))
        == lane_ids((PLANES * ROWS, 4 * LANES))
    ).astype(BF16)
    serving = first + row_ids((ROWS, PLANES)) - REACH
    parts = []
    for kind in range(2):
        d = odd if kind == 0 else 1 - odd
        for o in range(SPAN):
            total = jnp.zeros((ROWS, PLANES), F32)
            for k in range(4):
                hit = rows_ref[d, :, k] == serving + o
                total = total + jnp.where(hit, wts_ref[d, :, k], 0.0)
            total = total * (1.0 / CH)
            doubled = jnp.concatenate([total, jnp.zeros((ROWS, 64 - PLANES), F32)], axis=1)
            doubled = jnp.concatenate([doubled, doubled], axis=1)
            half = lane_ids(shape) >> 6
            parts.append(
                jnp.concatenate(
                    [jnp.where(row_ids(shape) == 2 * j + half, doubled, 0.0) for j in range(4)], axis=1
                )
            )
    table = jnp.concatenate(parts, axis=0)
    high = table.astype(BF16)
    low = (table - high.astype(F32)).astype(BF16)
    for n, piece in enumerate((high, low)):
        tab[n] = lax.dot_general(
            pick, piece, (((1,), (1,)), ((), ())), preferred_element_type=F32
        ).astype(BF16)

    for k in range(1, BANDS):
        s1_copy(peers[0], lax.rem(me + BANDS - k, BANDS)).wait_recv()

    column = lane_ids((1, LANES)) + me * STRIP - HALO
    inside = jnp.logical_and(column >= 0, column < COLS)

    def conv(x, t, pair):
        halves = []
        for b in (2 * pair, 2 * pair + 1):
            rows = x[BLK * b : BLK * b + KROWS].astype(F32)
            halves.append(
                jnp.concatenate([roll(rows, 2 - dx).astype(BF16) for dx in range(5)], axis=0)
            )
        return jnp.dot(t[...], jnp.concatenate(halves, axis=1), preferred_element_type=F32)

    def hidden(x, t, number, y, pair):
        out = conv(x, t, pair)
        for h in range(2):
            value = jnp.maximum(out[:, LANES * h : LANES * (h + 1)] + bias[number], 0.0)
            start = EDGE + BLK * (2 * pair + h)
            y[start : start + BLK] = jnp.where(inside, value, 0.0).astype(BF16)

    def f_copy(kind, b):
        return pltpu.make_async_remote_copy(
            src_ref=fblk.at[b],
            dst_ref=frx.at[kind, b],
            send_sem=f_send.at[kind, b],
            recv_sem=f_recv.at[kind, b],
            device_id=far if kind == 0 else near,
            device_id_type=MESH,
        )

    def o_copy(dst, strip):
        return pltpu.make_async_remote_copy(
            src_ref=fblk.at[dst],
            dst_ref=fback.at[strip],
            send_sem=o_send.at[dst],
            recv_sem=o_recv.at[strip],
            device_id=(cam, dst),
            device_id_type=MESH,
        )

    def last(pair):
        out = conv(x3, t3, pair)
        for h in range(2):
            b = 2 * pair + h
            value = out[:, LANES * h : LANES * (h + 1)] + bias[2]
            packed = jnp.concatenate(pack_features(value.reshape(CH, ROWS, LANES)), axis=0)
            packed = packed.astype(BF16)
            fblk[b] = packed
            fown[:, ROWS * b : ROWS * (b + 1)] = packed.astype(F32).reshape(GROUPS * PACK, ROWS, LANES)
            for kind in range(2):
                f_copy(kind, b).start()

            @pl.when(me != b)
            def _():
                o_copy(b, me).start()

    pairs = BANDS // 2
    for step in range(pairs + 2):
        if step < pairs:
            hidden(x1, t1, 0, x2, step)
        if 0 <= step - 1 < pairs:
            hidden(x2, t2, 1, x3, step - 1)
        if 0 <= step - 2 < pairs:
            last(step - 2)

    fback[me] = fblk[me]

    def m_copy(kind, dst, strip):
        return pltpu.make_async_remote_copy(
            src_ref=msend.at[kind, dst],
            dst_ref=mrecv.at[kind, strip],
            send_sem=m_send.at[kind, dst],
            recv_sem=m_recv.at[kind, strip],
            device_id=(cam, dst),
            device_id_type=MESH,
        )

    def arrive(kind, b):
        f_copy(kind, b).wait_recv()
        fpart[kind, :, ROWS * (b + 1) : ROWS * (b + 2)] = (
            frx[kind, b].astype(F32).reshape(GROUPS * PACK, ROWS, LANES)
        )

    lane = lane_ids((ROWS, LANES))

    def match(kind, b):
        def products(n, acc):
            own = fown[n, ROWS * b : ROWS * (b + 1)]
            return tuple(
                acc[o] + own * fpart[kind, n, ROWS * (b + 1) + o - REACH : ROWS * (b + 2) + o - REACH]
                for o in range(SPAN)
            )

        def group(g, accs):
            main, tail = accs
            for k in range(4):
                main = products(PACK * g + k, main)
            return main, products(PACK * g + 4, tail)

        zeros = tuple(jnp.zeros((ROWS, LANES), F32) for _ in range(SPAN))
        main, tail = lax.fori_loop(0, GROUPS, group, (zeros, zeros), unroll=2)
        main = [v + roll(v, 64) for v in main]
        for step in (64, 32, 16):
            tail = [v + roll(v, step) for v in tail]
        out = [jnp.where(lane < 64, main[2 * k], main[2 * k + 1]) for k in range(4)]
        ends = tail[0]
        for o in range(1, 8):
            ends = jnp.where(lane >= 16 * o, tail[o], ends)
        out.append(ends)
        out.append(jnp.where(lane < 64, main[8], tail[8]))
        msend[kind, b] = jnp.concatenate(out, axis=0).astype(BF16)

        @pl.when(me != b)
        def _():
            m_copy(kind, b, me).start()

    for kind in (1, 0):
        arrive(kind, 0)
        for b in range(BANDS):
            if b + 1 < BANDS:
                arrive(kind, b + 1)
            match(kind, b)
        mrecv[kind, me] = msend[kind, me]

    for k in range(1, BANDS):
        o_copy(peers[0], lax.rem(me + BANDS - k, BANDS)).wait_recv()
    for c in range(CH):
        g, k, h = c >> 3, (c & 7) >> 1, c & 1
        body = (PACK * g + k) * ROWS
        ends = (PACK * g + 4) * ROWS
        end_lane = 16 * k if h else 64 + 16 * k
        pieces = []
        for s in range(BANDS):
            pieces.append((lambda s=s: wide[s, body : body + ROWS], 64 * h, STRIP * s, 64))
            pieces.append((lambda s=s: wide[s, ends : ends + ROWS], end_lane, STRIP * s + 64, 16))
        if c == 0:
            for s in range(BANDS):
                wide[s] = fback[s].astype(F32)
        for t in range(TILES):
            featf[ROWS * c : ROWS * (c + 1), LANES * t : LANES * (t + 1)] = place(pieces, t)
    feat_ref[...] = featf[...].astype(BF16)

    for kind in (1, 0):
        for k in range(1, BANDS):
            m_copy(kind, peers[0], lax.rem(me + BANDS - k, BANDS)).wait_recv()
        for s in range(BANDS):
            wide[s, 0:MPACK] = mrecv[kind, s].astype(F32)
        for o in range(SPAN):
            body = 8 * (o >> 1) if o < 8 else 5 * ROWS
            body_lane = 64 * (o & 1) if o < 8 else 0
            ends = 4 * ROWS if o < 8 else 5 * ROWS
            end_lane = 16 * o if o < 8 else 64
            pieces = []
            for s in range(BANDS):
                pieces.append((lambda s=s: wide[s, body : body + ROWS], body_lane, STRIP * s, 64))
                pieces.append((lambda s=s: wide[s, ends : ends + ROWS], end_lane, STRIP * s + 64, 16))
            start = MROWS * kind + ROWS * o
            for t in range(TILES):
                mval[start : start + ROWS, LANES * t : LANES * (t + 1)] = place(pieces, t)
    values = mval[...].astype(BF16)
    out = jnp.dot(tab[0], values, preferred_element_type=F32)
    out = out + jnp.dot(tab[1], values, preferred_element_type=F32)
    vol_ref[...] = out.astype(BF16)

    for peer in peers:
        s1_copy(peer, me).wait_send()
        o_copy(peer, me).wait_send()
        for kind in range(2):
            m_copy(kind, peer, me).wait_send()
    for b in range(BANDS):
        for kind in range(2):
            f_copy(kind, b).wait_send()


def local(cams, events, conv_in, bias_in, conv_mid, bias_mid, tap_rows, tap_weights):
    dma = pltpu.SemaphoreType.DMA
    vmem = pl.BlockSpec(memory_space=pltpu.VMEM)
    padded = (BANDS * BLK + 2 * EDGE, LANES)
    taps = (BLK, 5 * KROWS)
    operands = (
        events.reshape(BLK, COLS),
        conv_in.transpose(2, 3, 0, 1),
        conv_mid.transpose(0, 3, 4, 1, 2),
        bias_in.reshape(1, CH),
        bias_mid,
        tap_rows.transpose(0, 2, 3, 1),
        tap_weights.transpose(0, 2, 3, 1),
    )
    vol, feat = pl.pallas_call(
        functools.partial(kernel, cams),
        out_shape=(
            jax.ShapeDtypeStruct((PLANES * ROWS, COLS), BF16),
            jax.ShapeDtypeStruct((BLK, COLS), BF16),
        ),
        in_specs=[pl.BlockSpec(memory_space=pltpu.HBM)] * 7,
        out_specs=(vmem, vmem),
        scratch_shapes=[
            *[pltpu.VMEM(operand.shape, operand.dtype) for operand in operands],
            pltpu.VMEM((BANDS, BLK, LANES), BF16),
            pltpu.VMEM(padded, BF16),
            pltpu.VMEM(padded, BF16),
            pltpu.VMEM(padded, BF16),
            pltpu.VMEM(taps, BF16),
            pltpu.VMEM(taps, BF16),
            pltpu.VMEM(taps, BF16),
            pltpu.VMEM((3, BLK, LANES), F32),
            pltpu.VMEM((BANDS, FROWS, LANES), BF16),
            pltpu.VMEM((2, BANDS, FROWS, LANES), BF16),
            pltpu.VMEM((GROUPS * PACK, ROWS * BANDS, LANES), F32),
            pltpu.VMEM((2, GROUPS * PACK, ROWS * (BANDS + 2), LANES), F32),
            pltpu.VMEM((BANDS, FROWS, LANES), BF16),
            pltpu.VMEM((2, BANDS, MPACK, LANES), BF16),
            pltpu.VMEM((2, BANDS, MPACK, LANES), BF16),
            pltpu.VMEM((2 * MROWS, COLS), F32),
            pltpu.VMEM((BLK, COLS), F32),
            pltpu.VMEM((BANDS, FROWS, LANES), F32),
            pltpu.VMEM((2, PLANES * ROWS, 2 * MROWS), BF16),
            dma((7,)),
            dma((BANDS,)), dma((BANDS,)),
            dma((2, BANDS)), dma((2, BANDS)),
            dma((BANDS,)), dma((BANDS,)),
            dma((2, BANDS)), dma((2, BANDS)),
        ],
        compiler_params=pltpu.CompilerParams(
            collective_id=0, has_side_effects=True, vmem_limit_bytes=64 * 1024 * 1024
        ),
    )(*operands)
    return vol.reshape(1, PLANES, ROWS, COLS), feat.reshape(1, CH, ROWS, COLS)


def solution(mesh):
    in_specs = (
        P("cam", None, "row", None),
        P(),
        P(),
        P(),
        P(),
        P(None, None, "row", None),
        P(None, None, "row", None),
    )
    out_specs = (P("cam", None, "row", None), P("cam", None, "row", None))
    return jax.shard_map(
        functools.partial(local, mesh.shape["cam"]),
        mesh=mesh,
        in_specs=in_specs,
        out_specs=out_specs,
        check_vma=False,
    )
```

time: 46.9 us -> 41.7 us (0.89)
  the two profiles are of different devices: /device:TPU:2 before, /device:TPU:24 now
where the time goes in v2:
time: 41.7 us; the launch traced here: 41.6 us
  Pallas kernels  38.3 us (92%)
  local copies, waits for them, and re-layouts  2.62 us (6%)
  between operations  0.65 us (2%)
    pallas_call x1, Pallas kernels, local(): pl.pallas_call(functools.partial(kernel, cams), out_shape=(jax.ShapeDtype...  38.3 us
    unnamed x4, local copies, waits for them, and re-layouts  2.62 us

profile of v2, /device:TPU:24, one launch (start us, length us, event | category | flops | bytes accessed | tf_op | source)
XLA Modules:
  0.0 41.6 jit_solution(6473750567704697181)
XLA Ops:
  0.6 38.3 %shard_map.86 = (bf16[384,640]{1,0:T(8,128)(2,1)}, bf16[256,640]{1,0:T(8,128)(2,1)}) custom-call(bf16[256,640]{1,0:T(8,128)(2,1)} %bitcast.10, bf16[5,5,32,32]{3,2,1,0:T(8,128)(2,1)} %bitcast.12, bf16[2,5,5,32,32]{4,3,2,1,0:T(8,128)(2,1)} %bitcast.9, f32[1,32]{1,0:T(1,128)} %bitcast.15, f32[2,32]{1,0:T(2,128)} %bm_hbm.1, s32[2,8,4,48]{3,2,1,0:T(4,128)} %bitcast.13, ...), custom_call_target="tpu_custom_call" | custom-call | tf_op jit(solution)/shard_map/pallas_call | solution.py:415
  38.9 0.0 copy-start
  39.0 1.9 %copy.11 = bf16[1,48,8,640]{3,2,1,0:T(8,128)(2,1)} copy(bf16[1,48,8,640]{3,2,1,0:T(8,128)(2,1)} %bitcast.8) | data formatting | bytes 983040
  40.9 0.0 copy-done
  40.9 0.7 %copy.12 = bf16[1,32,8,640]{3,2,1,0:T(8,128)(2,1)} copy(bf16[1,32,8,640]{3,2,1,0:T(8,128)(2,1)S(1)} %bitcast.11) | data formatting | bytes 655360
Async XLA Ops:
  38.9 1.9 %copy-start = (bf16[256,640]{1,0:T(8,128)(2,1)S(1)}, bf16[256,640]{1,0:T(8,128)(2,1)}, u32[]{:S(2)}) copy-start(bf16[256,640]{1,0:T(8,128)(2,1)} %get-tuple-element.5) | copy-start | bytes 983044

commit v3 on v2

--- a/solution.py
+++ b/solution.py
@@ -30,6 +30,8 @@
 PACK = 5
 FROWS = GROUPS * PACK * ROWS
 MPACK = 6 * ROWS
+QUARTER = BLK // 4
+WROWS = 3 * QUARTER
 
 
 def lane_ids(shape):
@@ -62,11 +64,40 @@
     first = start // LANES
     off = start - first * LANES
     shape = tiles[0].shape
-    low = roll(tiles[first], -off) if first >= 0 else jnp.zeros(shape, F32)
+    low = roll(tiles[first], -off) if first >= 0 else jnp.zeros(shape, BF16)
     if LANES - off >= STRIP + 2 * HALO:
         return low
-    high = roll(tiles[first + 1], -off) if first + 1 < TILES else jnp.zeros(shape, F32)
+    high = roll(tiles[first + 1], -off) if first + 1 < TILES else jnp.zeros(shape, BF16)
     return jnp.where(lane_ids(shape) < LANES - off, low, high)
+
+
+def pack_window(value):
+    lane = lane_ids((QUARTER, LANES))
+    parts = [value[QUARTER * g : QUARTER * (g + 1)] for g in range(4)]
+    pairs = [jnp.where(lane < 64, parts[g], roll(parts[g + 1], 64)) for g in (0, 2)]
+    tail = roll(parts[0], -64)
+    for g in range(1, 4):
+        tail = jnp.where(lane >= 32 * g, roll(parts[g], 32 * g - 64), tail)
+    return jnp.concatenate(pairs + [tail], axis=0)
+
+
+def unpack_window(packed):
+    lane = lane_ids((QUARTER, LANES))
+    tail = packed[2 * QUARTER :]
+    parts = []
+    for g in range(4):
+        pair = packed[QUARTER * (g // 2) : QUARTER * (g // 2 + 1)]
+        parts.append(jnp.where(lane < 64, roll(pair, 64 * (g & 1)), roll(tail, 64 - 32 * g)))
+    return jnp.concatenate(parts, axis=0)
+
+
+def fold(lane, step, even, odd):
+    clear = (lane & step) == 0
+    own = jnp.where(clear, even, odd)
+    other = jnp.where(clear, odd, even)
+    if step == 64:
+        return own + roll(other, 64)
+    return own + jnp.where(clear, roll(other, -step), roll(other, step))
 
 
 def place(pieces, tile):
@@ -116,7 +147,7 @@
     ev_hbm, w1_hbm, wm_hbm, b1_hbm, bm_hbm, rows_hbm, wts_hbm,
     vol_ref, feat_ref,
     ev_ref, w1_ref, wm_ref, b1_ref, bm_ref, rows_ref, wts_ref,
-    win, x1, x2, x3, t1, t2, t3, bias, fblk, frx, fown, fpart, fback, msend, mrecv, mval, featf, wide, tab,
+    win, wrecv, x1, x2, x3, t1, t2, t3, bias, fblk, frx, fown, fpart, fback, macc, msend, mrecv, mval, featf, wide, tab,
     in_sem, s1_send, s1_recv, f_send, f_recv, o_send, o_recv, m_send, m_recv,
 ):
     cam = lax.axis_index("cam")
@@ -145,19 +176,16 @@
     loads[0].wait()
 
     ev = jnp.dot(row_major_perm(), ev_ref[...], preferred_element_type=F32)
-    tiles = [ev[:, LANES * t : LANES * (t + 1)] for t in range(TILES)]
+    tiles = [ev[:, LANES * t : LANES * (t + 1)].astype(BF16) for t in range(TILES)]
     for strip in range(BANDS):
-        win[strip] = window_of(tiles, strip).astype(BF16)
+        win[strip] = pack_window(window_of(tiles, strip))
 
     pl.semaphore_wait(barrier, BANDS + 1)
-
-    def block_rows(b):
-        return pl.ds(pl.multiple_of(EDGE + b * BLK, EDGE), BLK)
 
     def s1_copy(dst, src_row):
         return pltpu.make_async_remote_copy(
             src_ref=win.at[dst],
-            dst_ref=x1.at[block_rows(src_row)],
+            dst_ref=wrecv.at[src_row],
             send_sem=s1_send.at[dst],
             recv_sem=s1_recv.at[src_row],
             device_id=(cam, dst),
@@ -166,15 +194,16 @@
 
     for peer in peers:
         s1_copy(peer, me).start()
-    x1[block_rows(me)] = win[me]
+    wrecv[me] = win[me]
 
     for load in loads[1:]:
         load.wait()
 
     zero_edge = jnp.zeros((EDGE, LANES), BF16)
     for x in (x1, x2, x3):
-        x[0:EDGE] = zero_edge
-        x[EDGE + BANDS * BLK :] = zero_edge
+        for dx in range(5):
+            x[dx, 0:EDGE] = zero_edge
+            x[dx, EDGE + BANDS * BLK :] = zero_edge
     build_taps(lambda dy, dx: w1_ref[dy, dx], t1)
     build_taps(lambda dy, dx: wm_ref[0, dy, dx], t2)
     build_taps(lambda dy, dx: wm_ref[1, dy, dx], t3)
@@ -228,21 +257,22 @@
     column = lane_ids((1, LANES)) + me * STRIP - HALO
     inside = jnp.logical_and(column >= 0, column < COLS)
 
+    def put(x, b, value):
+        for dx in range(5):
+            x[dx, EDGE + BLK * b : EDGE + BLK * (b + 1)] = roll(value, 2 - dx)
+
     def conv(x, t, pair):
-        halves = []
-        for b in (2 * pair, 2 * pair + 1):
-            rows = x[BLK * b : BLK * b + KROWS].astype(F32)
-            halves.append(
-                jnp.concatenate([roll(rows, 2 - dx).astype(BF16) for dx in range(5)], axis=0)
-            )
+        halves = [
+            jnp.concatenate([x[dx, BLK * b : BLK * b + KROWS] for dx in range(5)], axis=0)
+            for b in (2 * pair, 2 * pair + 1)
+        ]
         return jnp.dot(t[...], jnp.concatenate(halves, axis=1), preferred_element_type=F32)
 
     def hidden(x, t, number, y, pair):
         out = conv(x, t, pair)
         for h in range(2):
             value = jnp.maximum(out[:, LANES * h : LANES * (h + 1)] + bias[number], 0.0)
-            start = EDGE + BLK * (2 * pair + h)
-            y[start : start + BLK] = jnp.where(inside, value, 0.0).astype(BF16)
+            put(y, 2 * pair + h, jnp.where(inside, value, 0.0).astype(BF16))
 
     def f_copy(kind, b):
         return pltpu.make_async_remote_copy(
@@ -281,6 +311,8 @@
                 o_copy(b, me).start()
 
     pairs = BANDS // 2
+    for b in range(BANDS):
+        put(x1, b, unpack_window(wrecv[b]))
     for step in range(pairs + 2):
         if step < pairs:
             hidden(x1, t1, 0, x2, step)
@@ -307,8 +339,6 @@
             frx[kind, b].astype(F32).reshape(GROUPS * PACK, ROWS, LANES)
         )
 
-    lane = lane_ids((ROWS, LANES))
-
     def match(kind, b):
         def products(n, acc):
             own = fown[n, ROWS * b : ROWS * (b + 1)]
@@ -324,21 +354,28 @@
             return main, products(PACK * g + 4, tail)
 
         zeros = tuple(jnp.zeros((ROWS, LANES), F32) for _ in range(SPAN))
-        main, tail = lax.fori_loop(0, GROUPS, group, (zeros, zeros), unroll=2)
-        main = [v + roll(v, 64) for v in main]
+        accs = lax.fori_loop(0, GROUPS, group, (zeros, zeros), unroll=True)
+        for n in range(2):
+            for o in range(SPAN):
+                macc[n, o, ROWS * b : ROWS * (b + 1)] = accs[n][o]
+
+    def finish(kind, first):
+        count = ROWS * BANDS // 2
+        rows = slice(ROWS * first, ROWS * first + count)
+        lane = lane_ids((count, LANES))
+        main = [macc[0, o, rows] for o in range(SPAN)]
+        tail = [macc[1, o, rows] for o in range(SPAN)]
+        out = [fold(lane, 64, main[2 * k], main[2 * k + 1]) for k in range(4)]
+        ends = [fold(lane, 64, tail[o], tail[o + 4]) for o in range(4)]
+        ends = [fold(lane, 32, ends[o], ends[o + 2]) for o in range(2)]
+        out.append(fold(lane, 16, ends[0], ends[1]))
+        last_tail = tail[8]
         for step in (64, 32, 16):
-            tail = [v + roll(v, step) for v in tail]
-        out = [jnp.where(lane < 64, main[2 * k], main[2 * k + 1]) for k in range(4)]
-        ends = tail[0]
-        for o in range(1, 8):
-            ends = jnp.where(lane >= 16 * o, tail[o], ends)
-        out.append(ends)
-        out.append(jnp.where(lane < 64, main[8], tail[8]))
-        msend[kind, b] = jnp.concatenate(out, axis=0).astype(BF16)
-
-        @pl.when(me != b)
-        def _():
-            m_copy(kind, b, me).start()
+            last_tail = last_tail + roll(last_tail, step)
+        out.append(jnp.where(lane < 64, main[8] + roll(main[8], 64), last_tail))
+        for n in range(BANDS // 2):
+            part = [v[ROWS * n : ROWS * (n + 1)] for v in out]
+            msend[kind, first + n] = jnp.concatenate(part, axis=0).astype(BF16)
 
     for kind in (1, 0):
         arrive(kind, 0)
@@ -346,6 +383,10 @@
             if b + 1 < BANDS:
                 arrive(kind, b + 1)
             match(kind, b)
+        for first in (0, BANDS // 2):
+            finish(kind, first)
+        for peer in peers:
+            m_copy(kind, peer, me).start()
         mrecv[kind, me] = msend[kind, me]
 
     for k in range(1, BANDS):
@@ -401,7 +442,7 @@
 def local(cams, events, conv_in, bias_in, conv_mid, bias_mid, tap_rows, tap_weights):
     dma = pltpu.SemaphoreType.DMA
     vmem = pl.BlockSpec(memory_space=pltpu.VMEM)
-    padded = (BANDS * BLK + 2 * EDGE, LANES)
+    padded = (5, BANDS * BLK + 2 * EDGE, LANES)
     taps = (BLK, 5 * KROWS)
     operands = (
         events.reshape(BLK, COLS),
@@ -415,14 +456,15 @@
     vol, feat = pl.pallas_call(
         functools.partial(kernel, cams),
         out_shape=(
-            jax.ShapeDtypeStruct((PLANES * ROWS, COLS), BF16),
-            jax.ShapeDtypeStruct((BLK, COLS), BF16),
+            pltpu.VMEM((PLANES * ROWS, COLS), BF16),
+            pltpu.VMEM((BLK, COLS), BF16),
         ),
         in_specs=[pl.BlockSpec(memory_space=pltpu.HBM)] * 7,
         out_specs=(vmem, vmem),
         scratch_shapes=[
             *[pltpu.VMEM(operand.shape, operand.dtype) for operand in operands],
-            pltpu.VMEM((BANDS, BLK, LANES), BF16),
+            pltpu.VMEM((BANDS, WROWS, LANES), BF16),
+            pltpu.VMEM((BANDS, WROWS, LANES), BF16),
             pltpu.VMEM(padded, BF16),
             pltpu.VMEM(padded, BF16),
             pltpu.VMEM(padded, BF16),
@@ -435,6 +477,7 @@
             pltpu.VMEM((GROUPS * PACK, ROWS * BANDS, LANES), F32),
             pltpu.VMEM((2, GROUPS * PACK, ROWS * (BANDS + 2), LANES), F32),
             pltpu.VMEM((BANDS, FROWS, LANES), BF16),
+            pltpu.VMEM((2, SPAN, ROWS * BANDS, LANES), F32),
             pltpu.VMEM((2, BANDS, MPACK, LANES), BF16),
             pltpu.VMEM((2, BANDS, MPACK, LANES), BF16),
             pltpu.VMEM((2 * MROWS, COLS), F32),
@@ -448,9 +491,9 @@
             dma((2, BANDS)), dma((2, BANDS)),
         ],
         compiler_params=pltpu.CompilerParams(
-            collective_id=0, has_side_effects=True, vmem_limit_bytes=64 * 1024 * 1024
+            collective_id=0, has_side_effects=True, vmem_limit_bytes=48 * 1024 * 1024
         ),
-    )(*operands)
+    )(*[pltpu.with_memory_space_constraint(operand, pltpu.HBM) for operand in operands])
     return vol.reshape(1, PLANES, ROWS, COLS), feat.reshape(1, CH, ROWS, COLS)
 
 

time: 41.7 us -> 40.5 us (0.971)
  the two profiles are of different devices: /device:TPU:24 before, /device:TPU:2 now
where the time goes in v3:
time: 40.5 us; the launch traced here: 40.3 us
  Pallas kernels  38.2 us (94%)
  local copies, waits for them, and re-layouts  1.5 us (4%)
  between operations  0.64 us (2%)
    pallas_call x1, Pallas kernels, local(): pl.pallas_call(functools.partial(kernel, cams), out_shape=(pltpu.VMEM((PL...  38.2 us
    unnamed x2, local copies, waits for them, and re-layouts  1.5 us

profile of v3, /device:TPU:2, one launch (start us, length us, event | category | flops | bytes accessed | tf_op | source)
XLA Modules:
  0.0 40.3 jit_solution(11704580650884029323)
XLA Ops:
  0.6 38.2 %shard_map.86 = (bf16[384,640]{1,0:T(8,128)(2,1)S(1)}, bf16[256,640]{1,0:T(8,128)(2,1)S(1)}) custom-call(bf16[256,640]{1,0:T(8,128)(2,1)} %bitcast.11, bf16[5,5,32,32]{3,2,1,0:T(8,128)(2,1)} %bitcast.12, bf16[2,5,5,32,32]{4,3,2,1,0:T(8,128)(2,1)} %bitcast.10, f32[1,32]{1,0:T(1,128)} %bitcast.15, f32[2,32]{1,0:T(2,128)} %bm_hbm.1, s32[2,8,4,48]{3,2,1,0:T(4,128)} %bitcast.13, ...), custom_call_target="tpu_custom_call" | custom-call | tf_op jit(solution)/shard_map/pallas_call | solution.py:456
  38.8 0.8 %copy.11 = bf16[1,48,8,640]{3,2,1,0:T(8,128)(2,1)} copy(bf16[1,48,8,640]{3,2,1,0:T(8,128)(2,1)S(1)} %bitcast.8) | data formatting | bytes 983040
  39.6 0.7 %copy.12 = bf16[1,32,8,640]{3,2,1,0:T(8,128)(2,1)} copy(bf16[1,32,8,640]{3,2,1,0:T(8,128)(2,1)S(1)} %bitcast.9) | data formatting | bytes 655360

commit v4 on v3

--- a/solution.py
+++ b/solution.py
@@ -147,8 +147,8 @@
     ev_hbm, w1_hbm, wm_hbm, b1_hbm, bm_hbm, rows_hbm, wts_hbm,
     vol_ref, feat_ref,
     ev_ref, w1_ref, wm_ref, b1_ref, bm_ref, rows_ref, wts_ref,
-    win, wrecv, x1, x2, x3, t1, t2, t3, bias, fblk, frx, fown, fpart, fback, macc, msend, mrecv, mval, featf, wide, tab,
-    in_sem, s1_send, s1_recv, f_send, f_recv, o_send, o_recv, m_send, m_recv,
+    win, wrecv, x1, x2, x3, t1, t2, t3, bias, fblk, frx, fown, fpart, fback, macc, msend, mrecv, mval, volf, featf, wide, tab,
+    in_sem, s1_send, s1_recv, f_send, f_recv, o_send, o_recv, m_send, m_recv, seam_send, far_sem,
 ):
     cam = lax.axis_index("cam")
     me = lax.axis_index("row")
@@ -160,8 +160,21 @@
     barrier = pltpu.get_barrier_semaphore()
     for peer in peers:
         pl.semaphore_signal(barrier, inc=1, device_id=(cam, peer), device_id_type=MESH)
-    for peer in (far, near):
-        pl.semaphore_signal(barrier, inc=1, device_id=peer, device_id_type=MESH)
+    pl.semaphore_signal(barrier, inc=1, device_id=near, device_id_type=MESH)
+
+    place_in_run = lax.rem(cam, cams // 2)
+    late = place_in_run == cams // 2 - 1
+    early = place_in_run == 0
+
+    @pl.when(jnp.logical_not(late))
+    def _():
+        pl.semaphore_signal(barrier, inc=1, device_id=far, device_id_type=MESH)
+
+    @pl.when(early)
+    def _():
+        for peer in peers:
+            pl.semaphore_signal(barrier, inc=1, device_id=(far[0], peer), device_id_type=MESH)
+
     loads = [
         pltpu.make_async_copy(src, dst, in_sem.at[n])
         for n, (src, dst) in enumerate(
@@ -180,7 +193,8 @@
     for strip in range(BANDS):
         win[strip] = pack_window(window_of(tiles, strip))
 
-    pl.semaphore_wait(barrier, BANDS + 1)
+    expected = BANDS + 1 + (BANDS - 1) * late.astype(jnp.int32) - early.astype(jnp.int32)
+    pl.semaphore_wait(barrier, expected)
 
     def s1_copy(dst, src_row):
         return pltpu.make_async_remote_copy(
@@ -195,6 +209,11 @@
     for peer in peers:
         s1_copy(peer, me).start()
     wrecv[me] = win[me]
+
+    @pl.when(late)
+    def _():
+        pl.semaphore_signal(far_sem, inc=1, device_id=far, device_id_type=MESH)
+
 
     for load in loads[1:]:
         load.wait()
@@ -218,6 +237,8 @@
         edge = jnp.zeros((GROUPS * PACK, ROWS, LANES), F32)
         fpart[d, :, 0:ROWS] = edge
         fpart[d, :, ROWS * (BANDS + 1) :] = edge
+    fown[:, 0:ROWS] = edge
+    fown[:, ROWS * (BANDS + 1) :] = edge
 
     first = me * ROWS
     shape = (ROWS, LANES)
@@ -226,8 +247,8 @@
         == lane_ids((PLANES * ROWS, 4 * LANES))
     ).astype(BF16)
     serving = first + row_ids((ROWS, PLANES)) - REACH
-    parts = []
     for kind in range(2):
+        parts = []
         d = odd if kind == 0 else 1 - odd
         for o in range(SPAN):
             total = jnp.zeros((ROWS, PLANES), F32)
@@ -243,12 +264,11 @@
                     [jnp.where(row_ids(shape) == 2 * j + half, doubled, 0.0) for j in range(4)], axis=1
                 )
             )
-    table = jnp.concatenate(parts, axis=0)
-    high = table.astype(BF16)
-    low = (table - high.astype(F32)).astype(BF16)
-    for n, piece in enumerate((high, low)):
-        tab[n] = lax.dot_general(
-            pick, piece, (((1,), (1,)), ((), ())), preferred_element_type=F32
+        table = jnp.concatenate(parts, axis=0)
+        high = table.astype(BF16).astype(F32)
+        table = jnp.concatenate([high, table - high], axis=0).astype(BF16)
+        tab[kind] = lax.dot_general(
+            pick, table, (((1,), (1,)), ((), ())), preferred_element_type=F32
         ).astype(BF16)
 
     for k in range(1, BANDS):
@@ -302,12 +322,21 @@
             packed = jnp.concatenate(pack_features(value.reshape(CH, ROWS, LANES)), axis=0)
             packed = packed.astype(BF16)
             fblk[b] = packed
-            fown[:, ROWS * b : ROWS * (b + 1)] = packed.astype(F32).reshape(GROUPS * PACK, ROWS, LANES)
-            for kind in range(2):
-                f_copy(kind, b).start()
-
-            @pl.when(me != b)
-            def _():
+            fown[:, ROWS * (b + 1) : ROWS * (b + 2)] = packed.astype(F32).reshape(
+                GROUPS * PACK, ROWS, LANES
+            )
+
+        @pl.when(jnp.logical_not(late))
+        def _():
+            for h in range(2):
+                f_copy(0, 2 * pair + h).start()
+
+        for h in range(2):
+            f_copy(1, 2 * pair + h).start()
+        for h in range(2):
+
+            @pl.when(me != 2 * pair + h)
+            def _(b=2 * pair + h):
                 o_copy(b, me).start()
 
     pairs = BANDS // 2
@@ -318,6 +347,12 @@
             hidden(x1, t1, 0, x2, step)
         if 0 <= step - 1 < pairs:
             hidden(x2, t2, 1, x3, step - 1)
+        if step == 2:
+
+            @pl.when(early)
+            def _():
+                pl.semaphore_wait(far_sem, 1)
+
         if 0 <= step - 2 < pairs:
             last(step - 2)
 
@@ -339,11 +374,11 @@
             frx[kind, b].astype(F32).reshape(GROUPS * PACK, ROWS, LANES)
         )
 
-    def match(kind, b):
+    def match(own_ref, part_ref, b):
         def products(n, acc):
-            own = fown[n, ROWS * b : ROWS * (b + 1)]
+            own = own_ref[n, ROWS * (b + 1) : ROWS * (b + 2)]
             return tuple(
-                acc[o] + own * fpart[kind, n, ROWS * (b + 1) + o - REACH : ROWS * (b + 2) + o - REACH]
+                acc[o] + own * part_ref[n, ROWS * (b + 1) + o - REACH : ROWS * (b + 2) + o - REACH]
                 for o in range(SPAN)
             )
 
@@ -377,17 +412,52 @@
             part = [v[ROWS * n : ROWS * (n + 1)] for v in out]
             msend[kind, first + n] = jnp.concatenate(part, axis=0).astype(BF16)
 
-    for kind in (1, 0):
-        arrive(kind, 0)
+    def seam_copy(dst):
+        return pltpu.make_async_remote_copy(
+            src_ref=msend.at[2, dst],
+            dst_ref=mrecv.at[0, me],
+            send_sem=seam_send.at[dst],
+            recv_sem=m_recv.at[0, me],
+            device_id=(far[0], dst),
+            device_id_type=MESH,
+        )
+
+    @pl.when(late)
+    def _():
         for b in range(BANDS):
-            if b + 1 < BANDS:
-                arrive(kind, b + 1)
-            match(kind, b)
-        for first in (0, BANDS // 2):
-            finish(kind, first)
+            arrive(0, b)
+        for b in range(BANDS):
+            match(fpart.at[0], fown, b)
+        for first_block in (0, BANDS // 2):
+            finish(2, first_block)
+        for dst in range(BANDS):
+            seam_copy(dst).start()
+
+    arrive(1, 0)
+    for b in range(BANDS):
+        if b + 1 < BANDS:
+            arrive(1, b + 1)
+        match(fown, fpart.at[1], b)
+    for first_block in (0, BANDS // 2):
+        finish(1, first_block)
+    for peer in peers:
+        m_copy(1, peer, me).start()
+    mrecv[1, me] = msend[1, me]
+
+    @pl.when(jnp.logical_not(early))
+    def _():
+        @pl.when(jnp.logical_not(late))
+        def _():
+            for b in range(BANDS):
+                arrive(0, b)
+
+        for b in range(BANDS):
+            match(fown, fpart.at[0], b)
+        for first_block in (0, BANDS // 2):
+            finish(0, first_block)
         for peer in peers:
-            m_copy(kind, peer, me).start()
-        mrecv[kind, me] = msend[kind, me]
+            m_copy(0, peer, me).start()
+        mrecv[0, me] = msend[0, me]
 
     for k in range(1, BANDS):
         o_copy(peers[0], lax.rem(me + BANDS - k, BANDS)).wait_recv()
@@ -408,6 +478,12 @@
     feat_ref[...] = featf[...].astype(BF16)
 
     for kind in (1, 0):
+        if kind == 0:
+
+            @pl.when(early)
+            def _():
+                m_copy(0, peers[0], me).wait_recv()
+
         for k in range(1, BANDS):
             m_copy(kind, peers[0], lax.rem(me + BANDS - k, BANDS)).wait_recv()
         for s in range(BANDS):
@@ -421,22 +497,49 @@
             for s in range(BANDS):
                 pieces.append((lambda s=s: wide[s, body : body + ROWS], body_lane, STRIP * s, 64))
                 pieces.append((lambda s=s: wide[s, ends : ends + ROWS], end_lane, STRIP * s + 64, 16))
-            start = MROWS * kind + ROWS * o
+            start = ROWS * o
             for t in range(TILES):
                 mval[start : start + ROWS, LANES * t : LANES * (t + 1)] = place(pieces, t)
-    values = mval[...].astype(BF16)
-    out = jnp.dot(tab[0], values, preferred_element_type=F32)
-    out = out + jnp.dot(tab[1], values, preferred_element_type=F32)
-    vol_ref[...] = out.astype(BF16)
+        values = mval[...]
+        values = jnp.concatenate([values, values], axis=0).astype(BF16)
+        out = jnp.dot(tab[kind], values, preferred_element_type=F32)
+        if kind == 1:
+            volf[...] = out
+        else:
+            vol_ref[...] = (volf[...] + out).astype(BF16)
 
     for peer in peers:
         s1_copy(peer, me).wait_send()
         o_copy(peer, me).wait_send()
-        for kind in range(2):
-            m_copy(kind, peer, me).wait_send()
+        m_copy(1, peer, me).wait_send()
     for b in range(BANDS):
-        for kind in range(2):
-            f_copy(kind, b).wait_send()
+        f_copy(1, b).wait_send()
+
+    @pl.when(jnp.logical_not(early))
+    def _():
+        for peer in peers:
+            m_copy(0, peer, me).wait_send()
+
+    @pl.when(late)
+    def _():
+        for dst in range(BANDS):
+            seam_copy(dst).wait_send()
+
+    @pl.when(jnp.logical_not(late))
+    def _():
+        for b in range(BANDS):
+            f_copy(0, b).wait_send()
+
+
+def store(vol, feat, vol_out, feat_out, sem):
+    copies = [
+        pltpu.make_async_copy(vol, vol_out, sem.at[0]),
+        pltpu.make_async_copy(feat, feat_out, sem.at[1]),
+    ]
+    for copy in copies:
+        copy.start()
+    for copy in copies:
+        copy.wait()
 
 
 def local(cams, events, conv_in, bias_in, conv_mid, bias_mid, tap_rows, tap_weights):
@@ -474,13 +577,14 @@
             pltpu.VMEM((3, BLK, LANES), F32),
             pltpu.VMEM((BANDS, FROWS, LANES), BF16),
             pltpu.VMEM((2, BANDS, FROWS, LANES), BF16),
-            pltpu.VMEM((GROUPS * PACK, ROWS * BANDS, LANES), F32),
+            pltpu.VMEM((GROUPS * PACK, ROWS * (BANDS + 2), LANES), F32),
             pltpu.VMEM((2, GROUPS * PACK, ROWS * (BANDS + 2), LANES), F32),
             pltpu.VMEM((BANDS, FROWS, LANES), BF16),
             pltpu.VMEM((2, SPAN, ROWS * BANDS, LANES), F32),
+            pltpu.VMEM((3, BANDS, MPACK, LANES), BF16),
             pltpu.VMEM((2, BANDS, MPACK, LANES), BF16),
-            pltpu.VMEM((2, BANDS, MPACK, LANES), BF16),
-            pltpu.VMEM((2 * MROWS, COLS), F32),
+            pltpu.VMEM((MROWS, COLS), F32),
+            pltpu.VMEM((PLANES * ROWS, COLS), F32),
             pltpu.VMEM((BLK, COLS), F32),
             pltpu.VMEM((BANDS, FROWS, LANES), F32),
             pltpu.VMEM((2, PLANES * ROWS, 2 * MROWS), BF16),
@@ -489,11 +593,20 @@
             dma((2, BANDS)), dma((2, BANDS)),
             dma((BANDS,)), dma((BANDS,)),
             dma((2, BANDS)), dma((2, BANDS)),
+            dma((BANDS,)), pltpu.SemaphoreType.REGULAR,
         ],
         compiler_params=pltpu.CompilerParams(
             collective_id=0, has_side_effects=True, vmem_limit_bytes=48 * 1024 * 1024
         ),
     )(*[pltpu.with_memory_space_constraint(operand, pltpu.HBM) for operand in operands])
+    hbm = pl.BlockSpec(memory_space=pltpu.HBM)
+    vol, feat = pl.pallas_call(
+        store,
+        out_shape=(pltpu.HBM(vol.shape, BF16), pltpu.HBM(feat.shape, BF16)),
+        in_specs=[vmem, vmem],
+        out_specs=(hbm, hbm),
+        scratch_shapes=[dma((2,))],
+    )(*[pltpu.with_memory_space_constraint(value, pltpu.VMEM) for value in (vol, feat)])
     return vol.reshape(1, PLANES, ROWS, COLS), feat.reshape(1, CH, ROWS, COLS)
 
 

time: 40.5 us -> 35.5 us (0.88)
  the two profiles are of different devices: /device:TPU:2 before, /device:TPU:24 now
where the time goes in v4:
time: 35.5 us; the launch traced here: 35.2 us
  Pallas kernels  34.6 us (97%)
  between operations  0.64 us (2%)
    pallas_call x1, Pallas kernels, local(): pl.pallas_call(functools.partial(kernel, cams), out_shape=(pltpu.VMEM((PL...  33.7 us
    pallas_call x1, Pallas kernels, local(): pl.pallas_call(store, out_shape=(pltpu.HBM(vol.shape, BF16), pltpu.HBM(fe...  0.91 us

profile of v4, /device:TPU:24, one launch (start us, length us, event | category | flops | bytes accessed | tf_op | source)
XLA Modules:
  0.0 35.2 jit_solution(13093391536061511544)
XLA Ops:
  0.6 33.7 %shard_map.86 = (bf16[384,640]{1,0:T(8,128)(2,1)S(1)}, bf16[256,640]{1,0:T(8,128)(2,1)S(1)}) custom-call(bf16[256,640]{1,0:T(8,128)(2,1)} %bitcast.9, bf16[5,5,32,32]{3,2,1,0:T(8,128)(2,1)} %bitcast.10, bf16[2,5,5,32,32]{4,3,2,1,0:T(8,128)(2,1)} %bitcast.8, f32[1,32]{1,0:T(1,128)} %bitcast.13, f32[2,32]{1,0:T(2,128)} %bm_hbm.1, s32[2,8,4,48]{3,2,1,0:T(4,128)} %bitcast.11, ...), custom_call_target="tpu_custom_call" | custom-call | tf_op jit(solution)/shard_map/pallas_call | solution.py:559
  34.3 0.9 %shard_map.87 = (bf16[384,640]{1,0:T(8,128)(2,1)}, bf16[256,640]{1,0:T(8,128)(2,1)}) custom-call(bf16[384,640]{1,0:T(8,128)(2,1)S(1)} %get-tuple-element.6.vol, bf16[256,640]{1,0:T(8,128)(2,1)S(1)} %get-tuple-element.7.feat), custom_call_target="tpu_custom_call" | custom-call | tf_op jit(solution)/shard_map/pallas_call | solution.py:603

commit v5 on v4

--- a/solution.py
+++ b/solution.py
@@ -155,7 +155,13 @@
     odd = lax.rem(cam, 2)
     far = (lax.rem(cam + cams - 1 + 2 * odd, cams), me)
     near = (cam + 1 - 2 * odd, me)
-    peers = [lax.rem(me + k, BANDS) for k in range(1, BANDS)]
+    pair_of = lax.div(me, 2)
+    side = lax.rem(me, 2)
+
+    def row_at(dy, dx):
+        return 2 * lax.rem(pair_of + dy, BANDS // 2) + lax.rem(side + dx, 2)
+
+    peers = [row_at(dy, dx) for dy, dx in ((2, 1), (2, 0), (1, 1), (3, 1), (1, 0), (3, 0), (0, 1))]
 
     barrier = pltpu.get_barrier_semaphore()
     for peer in peers:
@@ -271,19 +277,16 @@
             pick, table, (((1,), (1,)), ((), ())), preferred_element_type=F32
         ).astype(BF16)
 
-    for k in range(1, BANDS):
-        s1_copy(peers[0], lax.rem(me + BANDS - k, BANDS)).wait_recv()
-
     column = lane_ids((1, LANES)) + me * STRIP - HALO
     inside = jnp.logical_and(column >= 0, column < COLS)
 
     def put(x, b, value):
         for dx in range(5):
-            x[dx, EDGE + BLK * b : EDGE + BLK * (b + 1)] = roll(value, 2 - dx)
+            x[dx, pl.ds(pl.multiple_of(EDGE + BLK * b, EDGE), BLK)] = roll(value, 2 - dx)
 
     def conv(x, t, pair):
         halves = [
-            jnp.concatenate([x[dx, BLK * b : BLK * b + KROWS] for dx in range(5)], axis=0)
+            jnp.concatenate([x[dx, pl.ds(pl.multiple_of(BLK * b, BLK), KROWS)] for dx in range(5)], axis=0)
             for b in (2 * pair, 2 * pair + 1)
         ]
         return jnp.dot(t[...], jnp.concatenate(halves, axis=1), preferred_element_type=F32)
@@ -333,28 +336,30 @@
 
         for h in range(2):
             f_copy(1, 2 * pair + h).start()
-        for h in range(2):
-
-            @pl.when(me != 2 * pair + h)
-            def _(b=2 * pair + h):
-                o_copy(b, me).start()
+
+    def take(r):
+        s1_copy(peers[0], r).wait_recv()
+        put(x1, r, unpack_window(wrecv[r]))
 
     pairs = BANDS // 2
-    for b in range(BANDS):
-        put(x1, b, unpack_window(wrecv[b]))
-    for step in range(pairs + 2):
-        if step < pairs:
-            hidden(x1, t1, 0, x2, step)
-        if 0 <= step - 1 < pairs:
-            hidden(x2, t2, 1, x3, step - 1)
-        if step == 2:
-
-            @pl.when(early)
-            def _():
-                pl.semaphore_wait(far_sem, 1)
-
-        if 0 <= step - 2 < pairs:
-            last(step - 2)
+    put(x1, me, unpack_window(wrecv[me]))
+    for dy, dx in ((0, 1), (1, 0), (3, 0), (1, 1), (3, 1)):
+        take(row_at(dy, dx))
+    hidden(x1, t1, 0, x2, pair_of)
+    for dx in range(2):
+        take(row_at(2, dx))
+    for k in range(1, pairs):
+        hidden(x1, t1, 0, x2, lax.rem(pair_of + k, pairs))
+
+    @pl.when(early)
+    def _():
+        pl.semaphore_wait(far_sem, 1)
+
+    for pair in range(pairs + 1):
+        if pair < pairs:
+            hidden(x2, t2, 1, x3, pair)
+        if pair > 0:
+            last(pair - 1)
 
     fback[me] = fblk[me]
 
@@ -426,12 +431,15 @@
     def _():
         for b in range(BANDS):
             arrive(0, b)
-        for b in range(BANDS):
-            match(fpart.at[0], fown, b)
         for first_block in (0, BANDS // 2):
+            for b in range(first_block, first_block + BANDS // 2):
+                match(fpart.at[0], fown, b)
             finish(2, first_block)
-        for dst in range(BANDS):
-            seam_copy(dst).start()
+            for dst in range(first_block, first_block + BANDS // 2):
+                seam_copy(dst).start()
+
+    for peer in peers:
+        o_copy(peer, me).start()
 
     arrive(1, 0)
     for b in range(BANDS):

time: 35.5 us -> 36.3 us (1.023)
  Pallas kernels: 34.6 us -> 35.4 us
    pallas_call x1, Pallas kernels: 33.7 us -> 34.5 us  [local(): pl.pallas_call(functools.partial(kernel, cams), out_shape=(pltpu.VMEM((PL...]
where the time goes in v5:
time: 36.3 us; the launch traced here: 36 us
  Pallas kernels  35.4 us (98%)
  between operations  0.64 us (2%)
    pallas_call x1, Pallas kernels, local(): pl.pallas_call(functools.partial(kernel, cams), out_shape=(pltpu.VMEM((PL...  34.5 us
    pallas_call x1, Pallas kernels, local(): pl.pallas_call(store, out_shape=(pltpu.HBM(vol.shape, BF16), pltpu.HBM(fe...  0.91 us

profile of v5, /device:TPU:24, one launch (start us, length us, event | category | flops | bytes accessed | tf_op | source)
XLA Modules:
  0.0 36.0 jit_solution(17068622785607034316)
XLA Ops:
  0.6 34.5 %shard_map.86 = (bf16[384,640]{1,0:T(8,128)(2,1)S(1)}, bf16[256,640]{1,0:T(8,128)(2,1)S(1)}) custom-call(bf16[256,640]{1,0:T(8,128)(2,1)} %bitcast.9, bf16[5,5,32,32]{3,2,1,0:T(8,128)(2,1)} %bitcast.10, bf16[2,5,5,32,32]{4,3,2,1,0:T(8,128)(2,1)} %bitcast.8, f32[1,32]{1,0:T(1,128)} %bitcast.13, f32[2,32]{1,0:T(2,128)} %bm_hbm.1, s32[2,8,4,48]{3,2,1,0:T(4,128)} %bitcast.11, ...), custom_call_target="tpu_custom_call" | custom-call | tf_op jit(solution)/shard_map/pallas_call | solution.py:567
  35.1 0.9 %shard_map.87 = (bf16[384,640]{1,0:T(8,128)(2,1)}, bf16[256,640]{1,0:T(8,128)(2,1)}) custom-call(bf16[384,640]{1,0:T(8,128)(2,1)S(1)} %get-tuple-element.6.vol, bf16[256,640]{1,0:T(8,128)(2,1)S(1)} %get-tuple-element.7.feat), custom_call_target="tpu_custom_call" | custom-call | tf_op jit(solution)/shard_map/pallas_call | solution.py:611

commit v6 on v4

--- a/solution.py
+++ b/solution.py
@@ -21,7 +21,9 @@
 TILES = COLS // LANES
 BLK = CH * ROWS
 EDGE = 2 * CH
-KROWS = BLK + 2 * EDGE
+GROUP = 4
+GBLK = GROUP * CH
+KROWS = GBLK + 2 * EDGE
 PLANES = 48
 SPAN = 9
 REACH = 4
@@ -54,9 +56,9 @@
 
 
 def channel_major_perm():
-    shape = (BLK, BLK)
+    shape = (GBLK, GBLK)
     i, j = row_ids(shape), lane_ids(shape)
-    return ((i & 7) * CH + (i >> 3) == j).astype(BF16)
+    return ((i & 3) * CH + (i >> 2) == j).astype(BF16)
 
 
 def window_of(tiles, strip):
@@ -111,14 +113,19 @@
     return out
 
 
-def pack_features(value):
+def pack_features(upper, lower):
+    upper = upper.reshape(CH // 2, ROWS, LANES)
+    lower = lower.reshape(CH // 2, ROWS, LANES)
+    first = lax.broadcasted_iota(jnp.int32, upper.shape, 1) < GROUP
+    evens = jnp.where(first, upper, pltpu.roll(lower, GROUP, 1))
+    odds = jnp.where(first, pltpu.roll(upper, GROUP, 1), lower)
     lane = lane_ids((ROWS, LANES))
     out = []
     for g in range(GROUPS):
         tail = None
         for k in range(4):
-            even = roll(value[8 * g + 2 * k], -HALO)
-            odd = roll(value[8 * g + 2 * k + 1], 64 - HALO)
+            even = roll(evens[4 * g + k], -HALO)
+            odd = roll(odds[4 * g + k], 64 - HALO)
             out.append(jnp.where(lane < 64, even, odd))
             both = roll(jnp.where(lane < 64, odd, even), 16 * k)
             tail = both if tail is None else jnp.where((lane & 63) >= 16 * k, both, tail)
@@ -130,16 +137,16 @@
     for dx in range(5):
         pieces = [w(dy, dx).astype(F32) for dy in range(5)]
         base = jnp.concatenate(pieces + [jnp.zeros((CH, KROWS - 5 * CH), F32)], axis=1)
-        for y in range(ROWS):
+        for y in range(GROUP):
             t_ref[CH * y : CH * (y + 1), KROWS * dx : KROWS * (dx + 1)] = roll(base, CH * y).astype(BF16)
 
 
 def bias_column(bias_row, channel_major):
-    shape = (BLK, CH)
+    shape = (GBLK, CH)
     i = row_ids(shape)
-    owner = (i >> 3) if channel_major else (i & 31)
+    owner = (i >> 2) if channel_major else (i & 31)
     spread = jnp.where(owner == lane_ids(shape), jnp.broadcast_to(bias_row, shape), 0.0)
-    return jnp.broadcast_to(jnp.sum(spread, axis=1, keepdims=True), (BLK, LANES))
+    return jnp.broadcast_to(jnp.sum(spread, axis=1, keepdims=True), (GBLK, LANES))
 
 
 def kernel(
@@ -155,7 +162,13 @@
     odd = lax.rem(cam, 2)
     far = (lax.rem(cam + cams - 1 + 2 * odd, cams), me)
     near = (cam + 1 - 2 * odd, me)
-    peers = [lax.rem(me + k, BANDS) for k in range(1, BANDS)]
+    pair_of = lax.div(me, 2)
+    side = lax.rem(me, 2)
+
+    def row_at(dy, dx):
+        return 2 * lax.rem(pair_of + dy, BANDS // 2) + lax.rem(side + dx, 2)
+
+    peers = [row_at(dy, dx) for dy, dx in ((2, 1), (2, 0), (1, 1), (3, 1), (1, 0), (3, 0), (0, 1))]
 
     barrier = pltpu.get_barrier_semaphore()
     for peer in peers:
@@ -271,28 +284,29 @@
             pick, table, (((1,), (1,)), ((), ())), preferred_element_type=F32
         ).astype(BF16)
 
-    for k in range(1, BANDS):
-        s1_copy(peers[0], lax.rem(me + BANDS - k, BANDS)).wait_recv()
-
     column = lane_ids((1, LANES)) + me * STRIP - HALO
     inside = jnp.logical_and(column >= 0, column < COLS)
 
-    def put(x, b, value):
+    def put(x, start, value):
+        start = pl.multiple_of(EDGE + start, EDGE)
         for dx in range(5):
-            x[dx, EDGE + BLK * b : EDGE + BLK * (b + 1)] = roll(value, 2 - dx)
+            x[dx, pl.ds(start, value.shape[0])] = roll(value, 2 - dx)
 
     def conv(x, t, pair):
-        halves = [
-            jnp.concatenate([x[dx, BLK * b : BLK * b + KROWS] for dx in range(5)], axis=0)
-            for b in (2 * pair, 2 * pair + 1)
-        ]
-        return jnp.dot(t[...], jnp.concatenate(halves, axis=1), preferred_element_type=F32)
+        out = []
+        for half in range(2):
+            cols = [
+                jnp.concatenate([x[dx, GBLK * g : GBLK * g + KROWS] for dx in range(5)], axis=0)
+                for g in (4 * pair + 2 * half, 4 * pair + 2 * half + 1)
+            ]
+            both = jnp.dot(t[...], jnp.concatenate(cols, axis=1), preferred_element_type=F32)
+            out += [both[:, :LANES], both[:, LANES:]]
+        return out
 
     def hidden(x, t, number, y, pair):
-        out = conv(x, t, pair)
-        for h in range(2):
-            value = jnp.maximum(out[:, LANES * h : LANES * (h + 1)] + bias[number], 0.0)
-            put(y, 2 * pair + h, jnp.where(inside, value, 0.0).astype(BF16))
+        for n, out in enumerate(conv(x, t, pair)):
+            value = jnp.maximum(out + bias[number], 0.0)
+            put(y, GBLK * (4 * pair + n), jnp.where(inside, value, 0.0).astype(BF16))
 
     def f_copy(kind, b):
         return pltpu.make_async_remote_copy(
@@ -318,8 +332,8 @@
         out = conv(x3, t3, pair)
         for h in range(2):
             b = 2 * pair + h
-            value = out[:, LANES * h : LANES * (h + 1)] + bias[2]
-            packed = jnp.concatenate(pack_features(value.reshape(CH, ROWS, LANES)), axis=0)
+            packed = pack_features(out[2 * h] + bias[2], out[2 * h + 1] + bias[2])
+            packed = jnp.concatenate(packed, axis=0)
             packed = packed.astype(BF16)
             fblk[b] = packed
             fown[:, ROWS * (b + 1) : ROWS * (b + 2)] = packed.astype(F32).reshape(
@@ -330,18 +344,24 @@
         def _():
             for h in range(2):
                 f_copy(0, 2 * pair + h).start()
+            for h in range(2):
+
+                @pl.when(me != 2 * pair + h)
+                def _(b=2 * pair + h):
+                    o_copy(b, me).start()
 
         for h in range(2):
             f_copy(1, 2 * pair + h).start()
-        for h in range(2):
-
-            @pl.when(me != 2 * pair + h)
-            def _(b=2 * pair + h):
-                o_copy(b, me).start()
+
+    def take(r):
+        s1_copy(peers[0], r).wait_recv()
+        put(x1, BLK * r, unpack_window(wrecv[r]))
+
+    put(x1, BLK * me, unpack_window(wrecv[me]))
+    for peer in reversed(peers):
+        take(peer)
 
     pairs = BANDS // 2
-    for b in range(BANDS):
-        put(x1, b, unpack_window(wrecv[b]))
     for step in range(pairs + 2):
         if step < pairs:
             hidden(x1, t1, 0, x2, step)
@@ -426,12 +446,15 @@
     def _():
         for b in range(BANDS):
             arrive(0, b)
-        for b in range(BANDS):
-            match(fpart.at[0], fown, b)
         for first_block in (0, BANDS // 2):
+            for b in range(first_block, first_block + BANDS // 2):
+                match(fpart.at[0], fown, b)
             finish(2, first_block)
-        for dst in range(BANDS):
-            seam_copy(dst).start()
+            for dst in range(first_block, first_block + BANDS // 2):
+                seam_copy(dst).start()
+
+        for peer in peers:
+            o_copy(peer, me).start()
 
     arrive(1, 0)
     for b in range(BANDS):
@@ -546,7 +569,7 @@
     dma = pltpu.SemaphoreType.DMA
     vmem = pl.BlockSpec(memory_space=pltpu.VMEM)
     padded = (5, BANDS * BLK + 2 * EDGE, LANES)
-    taps = (BLK, 5 * KROWS)
+    taps = (GBLK, 5 * KROWS)
     operands = (
         events.reshape(BLK, COLS),
         conv_in.transpose(2, 3, 0, 1),
@@ -574,7 +597,7 @@
             pltpu.VMEM(taps, BF16),
             pltpu.VMEM(taps, BF16),
             pltpu.VMEM(taps, BF16),
-            pltpu.VMEM((3, BLK, LANES), F32),
+            pltpu.VMEM((3, GBLK, LANES), F32),
             pltpu.VMEM((BANDS, FROWS, LANES), BF16),
             pltpu.VMEM((2, BANDS, FROWS, LANES), BF16),
             pltpu.VMEM((GROUPS * PACK, ROWS * (BANDS + 2), LANES), F32),

time: 35.5 us -> 32.9 us (0.927)
  Pallas kernels: 34.6 us -> 32.2 us
    pallas_call x1, Pallas kernels: 33.7 us -> 31.2 us  [local(): pl.pallas_call(functools.partial(kernel, cams), out_shape=(pltpu.VMEM((PL...]
where the time goes in v6:
time: 32.9 us; the launch traced here: 32.8 us
  Pallas kernels  32.2 us (98%)
  between operations  0.64 us (2%)
    pallas_call x1, Pallas kernels, local(): pl.pallas_call(functools.partial(kernel, cams), out_shape=(pltpu.VMEM((PL...  31.2 us
    pallas_call x1, Pallas kernels, local(): pl.pallas_call(store, out_shape=(pltpu.HBM(vol.shape, BF16), pltpu.HBM(fe...  0.91 us

profile of v6, /device:TPU:24, one launch (start us, length us, event | category | flops | bytes accessed | tf_op | source)
XLA Modules:
  0.0 32.8 jit_solution(10987230747640364885)
XLA Ops:
  0.6 31.2 %shard_map.86 = (bf16[384,640]{1,0:T(8,128)(2,1)S(1)}, bf16[256,640]{1,0:T(8,128)(2,1)S(1)}) custom-call(bf16[256,640]{1,0:T(8,128)(2,1)} %bitcast.9, bf16[5,5,32,32]{3,2,1,0:T(8,128)(2,1)} %bitcast.10, bf16[2,5,5,32,32]{4,3,2,1,0:T(8,128)(2,1)} %bitcast.8, f32[1,32]{1,0:T(1,128)} %bitcast.13, f32[2,32]{1,0:T(2,128)} %bm_hbm.1, s32[2,8,4,48]{3,2,1,0:T(4,128)} %bitcast.11, ...), custom_call_target="tpu_custom_call" | custom-call | tf_op jit(solution)/shard_map/pallas_call | solution.py:582
  31.9 0.9 %shard_map.87 = (bf16[384,640]{1,0:T(8,128)(2,1)}, bf16[256,640]{1,0:T(8,128)(2,1)}) custom-call(bf16[384,640]{1,0:T(8,128)(2,1)S(1)} %get-tuple-element.6.vol, bf16[256,640]{1,0:T(8,128)(2,1)S(1)} %get-tuple-element.7.feat), custom_call_target="tpu_custom_call" | custom-call | tf_op jit(solution)/shard_map/pallas_call | solution.py:626

commit v7 on v6

--- a/solution.py
+++ b/solution.py
@@ -178,6 +178,7 @@
     place_in_run = lax.rem(cam, cams // 2)
     late = place_in_run == cams // 2 - 1
     early = place_in_run == 0
+    defer = jnp.logical_or(place_in_run < 2, place_in_run >= cams // 2 - 2)
 
     @pl.when(jnp.logical_not(late))
     def _():
@@ -344,6 +345,9 @@
         def _():
             for h in range(2):
                 f_copy(0, 2 * pair + h).start()
+
+        @pl.when(jnp.logical_not(defer))
+        def _():
             for h in range(2):
 
                 @pl.when(me != 2 * pair + h)
@@ -453,6 +457,8 @@
             for dst in range(first_block, first_block + BANDS // 2):
                 seam_copy(dst).start()
 
+    @pl.when(defer)
+    def _():
         for peer in peers:
             o_copy(peer, me).start()
 

time: 32.9 us -> 32.9 us (level)
  no operation moved by 1% of the time
where the time goes in v7:
time: 32.9 us; the launch traced here: 32.8 us
  Pallas kernels  32.1 us (98%)
  between operations  0.64 us (2%)
    pallas_call x1, Pallas kernels, local(): pl.pallas_call(functools.partial(kernel, cams), out_shape=(pltpu.VMEM((PL...  31.2 us
    pallas_call x1, Pallas kernels, local(): pl.pallas_call(store, out_shape=(pltpu.HBM(vol.shape, BF16), pltpu.HBM(fe...  0.91 us

profile of v7, /device:TPU:24, one launch (start us, length us, event | category | flops | bytes accessed | tf_op | source)
XLA Modules:
  0.0 32.8 jit_solution(9205148923537525969)
XLA Ops:
  0.6 31.2 %shard_map.86 = (bf16[384,640]{1,0:T(8,128)(2,1)S(1)}, bf16[256,640]{1,0:T(8,128)(2,1)S(1)}) custom-call(bf16[256,640]{1,0:T(8,128)(2,1)} %bitcast.9, bf16[5,5,32,32]{3,2,1,0:T(8,128)(2,1)} %bitcast.10, bf16[2,5,5,32,32]{4,3,2,1,0:T(8,128)(2,1)} %bitcast.8, f32[1,32]{1,0:T(1,128)} %bitcast.13, f32[2,32]{1,0:T(2,128)} %bm_hbm.1, s32[2,8,4,48]{3,2,1,0:T(4,128)} %bitcast.11, ...), custom_call_target="tpu_custom_call" | custom-call | tf_op jit(solution)/shard_map/pallas_call | solution.py:588
  31.9 0.9 %shard_map.87 = (bf16[384,640]{1,0:T(8,128)(2,1)}, bf16[256,640]{1,0:T(8,128)(2,1)}) custom-call(bf16[384,640]{1,0:T(8,128)(2,1)S(1)} %get-tuple-element.6.vol, bf16[256,640]{1,0:T(8,128)(2,1)S(1)} %get-tuple-element.7.feat), custom_call_target="tpu_custom_call" | custom-call | tf_op jit(solution)/shard_map/pallas_call | solution.py:632

commit v8 on v6

--- a/solution.py
+++ b/solution.py
@@ -444,10 +444,9 @@
 
     @pl.when(late)
     def _():
-        for b in range(BANDS):
-            arrive(0, b)
         for first_block in (0, BANDS // 2):
             for b in range(first_block, first_block + BANDS // 2):
+                arrive(0, b)
                 match(fpart.at[0], fown, b)
             finish(2, first_block)
             for dst in range(first_block, first_block + BANDS // 2):

time: 32.9 us -> 33 us (level)
  no operation moved by 1% of the time
where the time goes in v8:
time: 33 us; the launch traced here: 32.8 us
  Pallas kernels  32.2 us (98%)
  between operations  0.64 us (2%)
    pallas_call x1, Pallas kernels, local(): pl.pallas_call(functools.partial(kernel, cams), out_shape=(pltpu.VMEM((PL...  31.3 us
    pallas_call x1, Pallas kernels, local(): pl.pallas_call(store, out_shape=(pltpu.HBM(vol.shape, BF16), pltpu.HBM(fe...  0.91 us

profile of v8, /device:TPU:24, one launch (start us, length us, event | category | flops | bytes accessed | tf_op | source)
XLA Modules:
  0.0 32.8 jit_solution(13693684785885829470)
XLA Ops:
  0.6 31.3 %shard_map.86 = (bf16[384,640]{1,0:T(8,128)(2,1)S(1)}, bf16[256,640]{1,0:T(8,128)(2,1)S(1)}) custom-call(bf16[256,640]{1,0:T(8,128)(2,1)} %bitcast.9, bf16[5,5,32,32]{3,2,1,0:T(8,128)(2,1)} %bitcast.10, bf16[2,5,5,32,32]{4,3,2,1,0:T(8,128)(2,1)} %bitcast.8, f32[1,32]{1,0:T(1,128)} %bitcast.13, f32[2,32]{1,0:T(2,128)} %bm_hbm.1, s32[2,8,4,48]{3,2,1,0:T(4,128)} %bitcast.11, ...), custom_call_target="tpu_custom_call" | custom-call | tf_op jit(solution)/shard_map/pallas_call | solution.py:581
  31.9 0.9 %shard_map.87 = (bf16[384,640]{1,0:T(8,128)(2,1)}, bf16[256,640]{1,0:T(8,128)(2,1)}) custom-call(bf16[384,640]{1,0:T(8,128)(2,1)S(1)} %get-tuple-element.6.vol, bf16[256,640]{1,0:T(8,128)(2,1)S(1)} %get-tuple-element.7.feat), custom_call_target="tpu_custom_call" | custom-call | tf_op jit(solution)/shard_map/pallas_call | solution.py:625
